TPU v7x, 512 devices: a whole 4x4x16 slice. The times are simulated.
512 devices in a mesh: ctx: 64 (over y, z), node: 4 (over x), tp: 2 (over core).
Axes of the slice: x: 4, y: 4, z: 16, core: 2. Of those that a mesh axis runs over, the one named last changes fastest.
Arguments:
- queries: bfloat16 [4, 8192, 1024], P('node', 'ctx', 'tp'), may hold values from -6 to 6
- key_vectors: bfloat16 [4, 8192, 1024], P('node', 'ctx', 'tp'), may hold values from -6 to 6
- value_vectors: bfloat16 [4, 8192, 2048], P('node', 'ctx', 'tp'), may hold values from -6 to 6
- decay_log: bfloat16 [4, 8192, 1024], P('node', 'ctx', 'tp'), may hold values from -16 to 0, as said below
- assignment: int32 [4, 64, 64], P('node'), may hold values from 0 to 4, as said below
- doc_lengths: int32 [8], replicated, may hold values from 1 to 24576, 32768 in all
- norm_gain: float32 [2048], P('tp'), may hold values from 0.5 to 1.5
Outputs:
- attended: bfloat16 [4, 8192, 2048], P('node', 'ctx', 'tp')
Inputs may be any that keep to these rules, and one draw needn't show every extreme that they name: `assignment`: in each node group's 64 x 64 matrix every row and every column sums to 128; an entry of 4 occurs in every node group. `decay_log`: logarithms of positive rates.
All inputs are finite; a program needn't handle non-finite values.
Results may differ from a plain program's by a relative error of at most 0.001.
Values may be sent and summed in bfloat16 or wider, within the bound.
No kernel may reach another device: no remote copies, remote signals or barrier semaphores. Data moves between devices by JAX's collectives and lax.ppermute only.
A program may use at most 128 MiB of HBM per device.

v0:
```python
import jax
import jax.numpy as jnp
from jax import lax
from jax.sharding import PartitionSpec as P

DK = 128


PRECISE = lax.Precision.HIGHEST
EPSILON = 1e-05


def entering(part, axis, combine, identity):
    place = lax.axis_index(axis)
    gathered = jax.tree.map(lambda a: lax.all_gather(a, axis), part)
    state = jax.tree.map(lambda a, e: jnp.zeros_like(a) + jnp.asarray(e, a.dtype), part, identity)

    def one(hop, state):
        return combine(
            state, jax.tree.map(lambda a: lax.dynamic_index_in_dim(a, hop, 0, False), gathered)
        )

    return lax.fori_loop(0, place, one, state)


def spread(block, axis, source):
    block = jnp.where(lax.axis_index(axis) == source, block, jnp.zeros_like(block))
    return lax.psum(block, axis)


def compose(earlier, later):
    return (earlier[0] * later[0], later[0][:, :, None] * earlier[1] + later[1])


def unpack(received, source_rows):
    flat_rows = received.reshape(-1, received.shape[2], received.shape[3])
    return jnp.take(flat_rows, source_rows, axis=0)


def block_work(received, source_rows, doc_ids, doc_before):
    query_f, key_f, value_f, rate_log = [
        unpack(stream, source_rows).astype(jnp.float32) for stream in received
    ]
    log_decay = -jnp.exp(rate_log)
    cumulative = jnp.cumsum(log_decay, axis=0)
    dec_query = query_f * jnp.exp(cumulative)
    inv_key = key_f * jnp.exp(-cumulative)
    scores = jnp.einsum("thc,shc->hts", dec_query, inv_key, precision=PRECISE)
    places = jnp.arange(doc_ids.shape[0], dtype=jnp.int32)
    allowed = (places[:, None] >= places[None, :]) & (doc_ids[:, None] == doc_ids[None, :])
    scores = jnp.where(allowed[None], scores, 0.0)
    local_out = jnp.einsum("hts,shv->htv", scores, value_f, precision=PRECISE)
    last_doc = (doc_ids == doc_ids[-1]).astype(jnp.float32)
    end_key = key_f * jnp.exp(cumulative[-1][None] - cumulative) * last_doc[:, None, None]
    fresh_state = jnp.einsum("shc,shv->hcv", end_key, value_f, precision=PRECISE)
    multiplier = jnp.exp(cumulative[-1]) * (doc_ids[-1] == doc_before).astype(jnp.float32)
    return (local_out, jnp.transpose(dec_query, (1, 0, 2)), multiplier, fresh_state)


def local(queries, key_vectors, value_vectors, decay_log, assignment, doc_lengths, norm_gain):
    ctx_count = lax.axis_size("ctx")
    own_index = lax.axis_index("ctx")
    node_index = lax.axis_index("node")
    row_count = queries.shape[1]
    head_count = queries.shape[2] // DK
    capacity = row_count // ctx_count + 2
    matrix = assignment[0]
    outgoing = lax.dynamic_index_in_dim(matrix, own_index, 0, keepdims=False)
    incoming = lax.dynamic_index_in_dim(matrix, own_index, 1, keepdims=False)
    src_start = jnp.cumsum(outgoing) - outgoing
    slots = jnp.arange(capacity, dtype=jnp.int32)
    picked = src_start[:, None] + slots[None, :]
    filled = slots[None, :] < outgoing[:, None]
    picked = jnp.clip(picked, 0, row_count - 1).reshape(-1)

    def pack(stream):
        shaped = stream[0].reshape(row_count, head_count, -1)
        taken = jnp.take(shaped, picked, axis=0).reshape(ctx_count, capacity, head_count, -1)
        return jnp.where(filled[:, :, None, None], taken, jnp.zeros_like(taken))

    packed_query = pack(queries)
    packed_key = pack(key_vectors)
    packed_value = pack(value_vectors)
    packed_rate = pack(decay_log)
    arrival_end = jnp.cumsum(incoming)
    arrival_start = arrival_end - incoming
    positions = jnp.arange(row_count, dtype=jnp.int32)
    source = jnp.sum((arrival_end[None, :] <= positions[:, None]).astype(jnp.int32), axis=1)
    onehot = (source[:, None] == jnp.arange(ctx_count, dtype=jnp.int32)[None, :]).astype(jnp.int32)
    offset = positions - jnp.sum(onehot * arrival_start[None, :], axis=1)
    source_rows = source * capacity + offset
    ends = jnp.cumsum(doc_lengths)
    first_place = (node_index * ctx_count + own_index) * row_count
    places = first_place + positions
    doc_ids = jnp.sum((ends[None, :] <= places[:, None]).astype(jnp.int32), axis=1)
    doc_before = jnp.sum((ends <= first_place - 1).astype(jnp.int32))
    received = (
        lax.all_to_all(packed_query, "ctx", split_axis=0, concat_axis=0, tiled=True),
        lax.all_to_all(packed_key, "ctx", split_axis=0, concat_axis=0, tiled=True),
        lax.all_to_all(packed_value, "ctx", split_axis=0, concat_axis=0, tiled=True),
        lax.all_to_all(packed_rate, "ctx", split_axis=0, concat_axis=0, tiled=True),
    )
    local_out, dec_query, multiplier, fresh_state = block_work(
        received, source_rows, doc_ids, doc_before
    )
    own_map = (multiplier, fresh_state)
    identity = (jnp.ones_like(multiplier), jnp.zeros_like(fresh_state))
    prefix = entering(own_map, "ctx", compose, identity)
    through = compose(prefix, own_map)
    group_map = (spread(through[0], "ctx", ctx_count - 1), spread(through[1], "ctx", ctx_count - 1))
    before_node = entering(group_map, "node", compose, identity)
    incoming_state = compose(before_node, prefix)[1]
    keep_mask = (doc_ids == doc_before).astype(jnp.float32)
    carried = (
        jnp.einsum("htc,hcv->htv", dec_query, incoming_state, precision=PRECISE)
        * keep_mask[None, :, None]
    )
    mixed = local_out + carried
    scale = lax.rsqrt(jnp.mean(mixed * mixed, axis=2, keepdims=True) + EPSILON)
    gains = norm_gain.reshape(head_count, -1)
    normed = mixed * scale * gains[:, None, :]
    return jnp.transpose(normed, (1, 0, 2)).reshape(1, row_count, -1).astype(jnp.bfloat16)


def solution(mesh):
    return jax.shard_map(
        local,
        mesh=mesh,
        in_specs=(
            P("node", "ctx", "tp"),
            P("node", "ctx", "tp"),
            P("node", "ctx", "tp"),
            P("node", "ctx", "tp"),
            P("node", None, None),
            P(),
            P("tp"),
        ),
        out_specs=P("node", "ctx", "tp"),
        check_vma=False,
    )
```

profile of v0, /device:TPU:6, one launch (start us, length us, event | category | flops | bytes accessed | tf_op | source)
XLA Modules:
  0.0 935.1 jit_solution(610413550171751533)
XLA Ops:
  6.5 0.7 fusion.24
  7.2 0.1 copy.31
  7.3 0.1 reduce-window.24
  7.4 0.1 reduce.2
  7.5 0.7 fusion.28
  8.2 0.1 add_clamp_fusion
  8.3 0.1 min.14
  8.5 0.9 reshape_squeeze.13
  9.4 0.9 reshape_squeeze.14
  10.3 1.0 gather_fusion.4
  11.3 1.0 gather_fusion.6
  12.3 0.9 reshape_squeeze.12
  13.3 1.0 gather_fusion.2
  14.3 0.1 iota_compare_fusion.3
  14.3 1.0 broadcast_select_fusion.2
  15.3 1.2 broadcast_select_fusion.6
  16.6 39.5 %all_to_all.20 = bf16[64,4,4,128]{3,2,1,0:T(4,128)(2,1)S(1)} all-to-all(bf16[64,4,4,128]{3,2,1,0:T(4,128)(2,1)S(1)} %get-tuple-element.126), channel_id=1, replica_groups=mesh['ctx'=64,'node'=4,'tp'=2] {'ctx'}, dimensions={0} | all-to-all | bytes 524288 | tf_op jit(solution)/shard_map/all_to_all | solution.py:101
  56.1 26.5 %all_to_all.21 = bf16[64,4,4,128]{3,2,1,0:T(4,128)(2,1)S(1)} all-to-all(bf16[64,4,4,128]{3,2,1,0:T(4,128)(2,1)S(1)} %get-tuple-element.127), channel_id=1, replica_groups=mesh['ctx'=64,'node'=4,'tp'=2] {'ctx'}, dimensions={0} | all-to-all | bytes 524288 | tf_op jit(solution)/shard_map/all_to_all | solution.py:99
  82.6 6.4 all-to-all-start
  89.0 0.1 min.15
  89.1 0.9 dynamic-slice_reduce_fusion
  90.0 0.1 reduce-window.25
  90.1 0.1 reduce
  90.3 0.8 reduce-window.23
  91.1 1.1 reshape_squeeze.15
  92.3 1.2 gather_fusion
  93.4 1.4 select_select_fusion
  94.9 13.7 %all-to-all-done = bf16[64,4,4,128]{3,2,1,0:T(4,128)(2,1)S(1)} async-done(((bf16[64,4,4,128]{3,2,1,0:T(4,128)(2,1)}), bf16[64,4,4,128]{3,2,1,0:T(4,128)(2,1)S(1)}, u32[]{:S(2)}, u32[]{:S(2)}) %all-to-all-start) | async-done | bytes 262176 | tf_op jit(solution)/shard_map/all_to_all | solution.py:98
  108.6 6.5 all-to-all-start.3
  115.1 0.1 convert_reduce_fusion.1
  115.2 0.6 slice.9
  115.8 0.7 fusion.21
  117.9 0.1 convert_reduce_fusion
  118.0 0.1 select_reduce_fusion
  118.1 1.3 compare_convert_fusion
  119.5 0.7 gather_fusion.5
  120.2 0.7 gather_fusion.7
  121.0 0.7 gather_fusion.3
  121.7 0.2 fusion.11
  121.9 0.4 convert_multiply_fusion.1
  122.3 22.5 %all-to-all-done.3 = bf16[64,4,4,256]{3,2,1,0:T(4,128)(2,1)S(1)} async-done(((bf16[64,4,4,256]{3,2,1,0:T(4,128)(2,1)}), bf16[64,4,4,256]{3,2,1,0:T(4,128)(2,1)S(1)}, u32[]{:S(2)}, u32[]{:S(2)}) %all-to-all-start.3) | async-done | bytes 524320 | tf_op jit(solution)/shard_map/all_to_all | solution.py:100
  144.9 0.8 gather_fusion.1
  145.7 0.2 broadcast_select_fusion.3
  145.9 1.2 fusion.6
  147.2 0.0 all-reduce.2.cloned.1.call-start
  147.2 99.0 %all_gather.22 = f32[64,4,128]{2,1,0:T(4,128)S(1)} all-gather(f32[1,4,128]{2,1,0:T(4,128)S(1)} %get-tuple-element.122), channel_id=1, replica_groups=mesh['ctx'=64,'node'=4,'tp'=2] {'ctx'}, dimensions={0}, use_global_device_ids=true | all-gather | bytes 133120 | tf_op jit(solution)/shard_map/all_gather | solution.py:15
  246.2 188.3 %all-gather.6.cloned.1.call-done = f32[256,128,256]{2,1,0:T(8,128)} async-done(((f32[4,128,256]{2,1,0:T(8,128)}), f32[256,128,256]{2,1,0:T(8,128)}) %all-gather.6.cloned.1.call-update) | async-done | bytes 33554448 | tf_op jit(solution)/shard_map/all_gather | solution.py:15
  434.6 2.0 select_bitcast_fusion
  436.6 0.0 all-gather.4.cloned.1.call-start
  436.7 334.5 %all-reduce.2.cloned.1.call-done = f32[1,4,128,256]{3,2,1,0:T(8,128)} async-done(((f32[1,4,128,256]{3,2,1,0:T(8,128)}), f32[1,4,128,256]{3,2,1,0:T(8,128)}) %all-reduce.2.cloned.1.call-update) | async-done | bytes 524304 | tf_op jit(solution)/shard_map/psum | solution.py:28
  771.2 0.7 mul.168
  771.9 0.1 fusion.20
  772.0 0.7 convolution_select_fusion
  772.7 139.7 %psum.14 = f32[1,4,128]{2,1,0:T(4,128)S(1)} all-reduce(f32[1,4,128]{2,1,0:T(4,128)S(1)} %get-tuple-element.112), channel_id=1, replica_groups=mesh['ctx'=64,'node'=4,'tp'=2] {'ctx'}, use_global_device_ids=true, to_apply=%region_10.13 | all-reduce | flops 512 | bytes 4096 | tf_op jit(solution)/shard_map/psum | solution.py:28
  912.3 10.1 %all_gather.26 = f32[4,4,128]{2,1,0:T(4,128)S(1)} all-gather(f32[1,4,128]{2,1,0:T(4,128)S(1)} %psum.14), channel_id=1, replica_groups=mesh['ctx'=64,'node'=4,'tp'=2] {'node'}, dimensions={0}, use_global_device_ids=true | all-gather | bytes 10240 | tf_op jit(solution)/shard_map/all_gather | solution.py:15
  922.5 3.8 while.25
  922.5 1.2 bitcast_add_fusion.5
  923.8 1.2 bitcast_add_fusion.5
  925.0 1.2 bitcast_add_fusion.5
  926.2 0.7 convolution_multiply_fusion
  927.0 0.5 multiply_reduce_fusion
  927.4 0.1 fusion.1
  927.6 0.2 copy.38
  927.7 0.9 copy.39
  (26 shorter events, 0.3 us)
Async XLA Ops:
  82.6 26.0 %all-to-all-start = ((bf16[64,4,4,128]{3,2,1,0:T(4,128)(2,1)}), bf16[64,4,4,128]{3,2,1,0:T(4,128)(2,1)S(1)}, u32[]{:S(2)}, u32[]{:S(2)}) async-start(bf16[64,4,4,128]{3,2,1,0:T(4,128)(2,1)} %get-tuple-element.125), calls=%async_computation | async-start | bytes 524288 | tf_op jit(solution)/shard_map/all_to_all | solution.py:98
  108.6 36.3 %all-to-all-start.3 = ((bf16[64,4,4,256]{3,2,1,0:T(4,128)(2,1)}), bf16[64,4,4,256]{3,2,1,0:T(4,128)(2,1)S(1)}, u32[]{:S(2)}, u32[]{:S(2)}) async-start(bf16[64,4,4,256]{3,2,1,0:T(4,128)(2,1)} %select_select_fusion), calls=%async_computation.3 | async-start | bytes 1048576 | tf_op jit(solution)/shard_map/all_to_all | solution.py:100
  115.1 319.5 %all-gather.6.cloned.1.call-start = ((), (), s32[]{:S(2)}) async-start(), calls=%async_computation.6 | async-start | bytes 34078720 | tf_op jit(solution)/shard_map/all_gather | solution.py:15
  147.2 624.0 %all-reduce.2.cloned.1.call-start = ((), (), s32[]{:S(2)}) async-start(), calls=%async_computation.4 | async-start | bytes 1048576 | tf_op jit(solution)/shard_map/psum | solution.py:28
  436.6 485.8 %all-gather.4.cloned.1.call-start = ((), (), s32[]{:S(2)}) async-start(), calls=%async_computation.5 | async-start | bytes 2621440 | tf_op jit(solution)/shard_map/all_gather | solution.py:15
Sparse Core Ops, SparseCore 0:
  147.3 287.1 all-gather.5
  438.0 333.1 all-reduce.1
  773.5 31.0 all-gather.3
where the time goes:
time: 939 us; the launch traced here: 935 us
  waiting for transfers between devices  559 us (60%)
  blocking collectives  315 us (34%)
  local copies, waits for them, and re-layouts  15.5 us (2%)
  other arithmetic  14.8 us (2%)
  between operations  14.8 us (2%)
  starting transfers between devices  13 us (1%)
    psum x1, waiting for transfers between devices, spread(): return lax.psum(block, axis)  335 us
    all_gather x2, waiting for transfers between devices, entering(): gathered = jax.tree.map(lambda a: lax.all_gather(a, axis), part)  188 us
    psum x1, blocking collectives, spread(): return lax.psum(block, axis)  140 us
    all_gather x2, blocking collectives, entering(): gathered = jax.tree.map(lambda a: lax.all_gather(a, axis), part)  109 us
    all_to_all x1, blocking collectives, local(): lax.all_to_all(packed_rate, 'ctx', split_axis=0, concat_axis=0, tiled=True)  39.5 us
    all_to_all x1, blocking collectives, local(): lax.all_to_all(packed_key, 'ctx', split_axis=0, concat_axis=0, tiled=True)  26.5 us
    all_to_all x1, waiting for transfers between devices, local(): lax.all_to_all(packed_value, 'ctx', split_axis=0, concat_axis=0, tiled=True)  22.5 us
  transfers between devices with their start and end apart: 5, of which 4 were waited for; matrix products, arithmetic and copies ran while one was open for 1% of the time, Pallas kernels for 0%

commit v1 on v0

v1 whole, which is shorter than its diff:
```python
import functools

import jax
import jax.numpy as jnp
from jax import lax
from jax.experimental import pallas as pl
from jax.experimental.pallas import tpu as pltpu
from jax.sharding import Mesh, PartitionSpec as P

DK = 128
DV = 256
HEADS = 4
GROUP = 4
TOK = 128
CAP = 16
CHUNK = GROUP * TOK
OWNERS = 64
WIDTH = 3 * DK + DV
EPSILON = 1e-05
CTX = ("y", "zh", "zl")
CHUNKS = ("node", "y", "zh")
PRECISE = lax.Precision.HIGHEST
F32 = jnp.float32
BF16 = jnp.bfloat16


def iota(shape, dim):
    return lax.broadcasted_iota(jnp.int32, shape, dim)


def dot(a, b, dims=((1,), (0,)), precision=None):
    return lax.dot_general(a, b, (dims, ((), ())), precision=precision, preferred_element_type=F32)


def pack_kernel(place_ref, matrix_ref, query_ref, key_ref, value_ref, rate_ref, out_ref):
    slots = (OWNERS // GROUP) * CAP
    counts = matrix_ref[pl.ds(place_ref[0], 1), :].astype(F32)
    chunk = lax.shift_right_logical(iota((slots, OWNERS), 0), 4)
    before = iota((slots, OWNERS), 1) < chunk * GROUP
    start = jnp.sum(jnp.where(before, counts, 0.0), axis=1, keepdims=True).astype(jnp.int32)
    wanted = start + (iota((slots, 1), 0) & (CAP - 1))
    pick = (iota((slots, TOK), 1) == wanted).astype(F32).astype(BF16)
    at = 0
    for ref, width in ((query_ref, DK), (key_ref, DK), (value_ref, DV), (rate_ref, DK)):
        rows = dot(pick, ref[...]).astype(BF16)
        for head in range(HEADS):
            piece = rows[:, head * width : (head + 1) * width]
            out_ref[:, head, :, at : at + width] = piece.reshape(slots // CAP, CAP, width)
        at += width


def doc_of(lengths_ref, places):
    end = jnp.int32(0)
    doc = jnp.zeros_like(places)
    for d in range(lengths_ref.shape[0]):
        end = end + lengths_ref[d]
        doc = doc + (end <= places).astype(jnp.int32)
    return doc


def unpack(place_ref, matrix_ref, received_ref):
    first = place_ref[1] * GROUP
    matrix = matrix_ref[...].astype(F32).astype(BF16)
    owner = iota((8, OWNERS), 1)
    nth = iota((8, OWNERS), 0)
    one = ((owner == first + nth) & (nth < GROUP)).astype(F32).astype(BF16)
    upto = ((owner >= first) & (owner <= first + nth) & (nth < GROUP)).astype(F32).astype(BF16)
    counts = dot(one, matrix, ((1,), (1,)))
    ends = dot(upto, matrix, ((1,), (1,)))
    earlier = (iota((OWNERS, OWNERS), 0) < iota((OWNERS, OWNERS), 1)).astype(F32).astype(BF16)
    arrive = dot(counts.astype(BF16), earlier)
    slots = OWNERS * CAP
    expand = (lax.shift_right_logical(iota((OWNERS, slots), 1), 4) == iota((OWNERS, slots), 0)).astype(F32).astype(BF16)
    counts, ends, arrive = [dot(a.astype(BF16), expand) for a in (counts, ends, arrive)]
    slot = (iota((8, slots), 1) & (CAP - 1)).astype(F32)
    inside = (slot < ends) & (slot >= ends - counts)
    target = iota((8, slots), 0).astype(F32) * TOK + arrive + slot - (ends - counts) + 1.0
    target = jnp.sum(jnp.where(inside, target, 0.0), axis=0, keepdims=True).astype(jnp.int32) - 1
    pick = (iota((CHUNK, slots), 0) == target).astype(F32).astype(BF16)
    return dot(pick, received_ref[...].reshape(slots, WIDTH))


def column(row):
    return jnp.transpose(jnp.broadcast_to(row, (DK, DK)))


def chunk_kernel(
    place_ref, lengths_ref, matrix_ref, received_ref, map_ref, partial_ref, query_out_ref
):
    rows = unpack(place_ref, matrix_ref, received_ref)
    first = (place_ref[2] * (OWNERS // GROUP) + place_ref[1]) * CHUNK
    tril = (iota((TOK, TOK), 0) >= iota((TOK, TOK), 1)).astype(F32)
    state = None
    passed = jnp.zeros((1, DK), F32)
    chunk_before = doc_of(lengths_ref, jnp.full((1, 1), first - 1, jnp.int32))
    for block in range(GROUP):
        here = rows[block * TOK : (block + 1) * TOK]
        query, key = here[:, :DK], here[:, DK : 2 * DK]
        value, rate = here[:, 2 * DK : 2 * DK + DV], here[:, 2 * DK + DV :]
        start = first + block * TOK
        doc_rows = doc_of(lengths_ref, start + iota((TOK, DK), 0))
        doc_columns = doc_of(lengths_ref, start + iota((TOK, TOK), 1))
        doc_before = doc_of(lengths_ref, jnp.full((1, 1), start - 1, jnp.int32))
        doc_last = doc_of(lengths_ref, jnp.full((1, 1), start + TOK - 1, jnp.int32))
        cumulative = dot(tril, -jnp.exp(rate), precision=PRECISE)
        whole = cumulative[TOK - 1 :, :]
        half = 0.5 * whole
        scores = dot(
            query * jnp.exp(cumulative - half),
            key * jnp.exp(half - cumulative),
            ((1,), (1,)),
            PRECISE,
        )
        allowed = (iota((TOK, TOK), 0) >= iota((TOK, TOK), 1)) & (doc_rows == doc_columns)
        out = dot(jnp.where(allowed, scores, 0.0), value, precision=PRECISE)
        if block > 0:
            kept = jnp.where(doc_rows == doc_before, query * jnp.exp(cumulative), 0.0)
            out = out + dot(kept, state, precision=PRECISE)
        span = slice(block * TOK, (block + 1) * TOK)
        partial_ref[span, :] = out
        query_out_ref[span, :] = jnp.where(
            doc_rows == chunk_before, query * jnp.exp(cumulative + passed), 0.0
        )
        end_key = jnp.where(doc_rows == doc_last, key * jnp.exp(whole - cumulative), 0.0)
        fresh = dot(end_key, value, ((0,), (0,)), PRECISE)
        if block == 0:
            state = fresh
        else:
            kept = column(jnp.where(doc_last == doc_before, jnp.exp(whole), 0.0))
            state = jnp.concatenate([kept, kept], axis=1) * state + fresh
        passed = passed + whole
    kept = column(jnp.where(doc_last == chunk_before, jnp.exp(passed), 0.0))
    low = iota((DK, DK), 1) < DK // 2
    for part in range(4):
        piece = state[:, (part // 2) * DK : (part // 2 + 1) * DK]
        if part % 2:
            piece = pltpu.roll(piece, DK // 2, 1)
        piece = jnp.where(low, piece, kept)
        map_ref[part * 16 : (part + 1) * 16] = piece.reshape(16, 8, DK)


def scan_kernel(map_ref, prefix_ref):
    low = iota(map_ref.shape[1:], 1) < DK // 2

    def step(chunk, state):
        prefix_ref[chunk] = state
        here = map_ref[chunk]
        return jnp.where(low, pltpu.roll(here, DK // 2, 1), 0.0) * state + here

    lax.fori_loop(0, map_ref.shape[0], step, jnp.zeros(map_ref.shape[1:], F32), unroll=True)


def finish_kernel(place_ref, prefix_ref, partial_ref, query_ref, gain_ref, out_ref):
    low = iota((DK, DK), 1) < DK // 2
    parts = [prefix_ref[part * 16 : (part + 1) * 16].reshape(DK, DK) for part in range(4)]
    state = jnp.concatenate(
        [
            jnp.where(low, parts[2 * side], pltpu.roll(parts[2 * side + 1], DK // 2, 1))
            for side in range(2)
        ],
        axis=1,
    )
    gain = gain_ref[pl.ds(place_ref[3], 1), :]
    for block in range(GROUP):
        span = slice(block * TOK, (block + 1) * TOK)
        mixed = partial_ref[span, :] + dot(query_ref[span, :], state, precision=PRECISE)
        scale = lax.rsqrt(jnp.mean(mixed * mixed, axis=1, keepdims=True) + EPSILON)
        out_ref[block] = (mixed * scale * gain).astype(BF16)


SMEM = pl.BlockSpec(memory_space=pltpu.SMEM)
VMEM = pl.BlockSpec(memory_space=pltpu.VMEM)


def call(kernel, scalars, arrays, outs, cost=0):
    return pl.pallas_call(
        kernel,
        out_shape=outs,
        in_specs=[SMEM] * scalars + [VMEM] * arrays,
        out_specs=jax.tree.map(lambda _: VMEM, outs),
        compiler_params=pltpu.CompilerParams(vmem_limit_bytes=32 << 20),
        cost_estimate=pl.CostEstimate(flops=cost, bytes_accessed=1 << 20, transcendentals=0),
    )


def shape(dims, dtype=F32):
    return jax.ShapeDtypeStruct(dims, dtype)


def local(queries, key_vectors, value_vectors, decay_log, assignment, doc_lengths, norm_gain):
    own = lax.axis_index(CTX)
    place = jnp.stack([own, own // GROUP, lax.axis_index("node"), own % GROUP]).astype(jnp.int32)
    matrix = assignment[0]
    packed = call(pack_kernel, 1, 5, shape((OWNERS // GROUP, HEADS, CAP, WIDTH), BF16), 1 << 28)(
        place, matrix, queries[0], key_vectors[0], value_vectors[0], decay_log[0]
    )
    received = lax.all_to_all(packed.reshape(OWNERS, CAP, WIDTH), CTX, 0, 0, tiled=True)
    maps, partial, query = call(
        chunk_kernel,
        2,
        2,
        (shape((OWNERS, 8, DK)), shape((CHUNK, DV)), shape((CHUNK, DK))),
        1 << 30,
    )(place, doc_lengths, matrix, received)
    maps = lax.all_to_all(maps, CHUNKS, 0, 0, tiled=True)
    prefix = call(scan_kernel, 0, 1, shape((OWNERS, 8, DK)), 1 << 24)(maps)
    prefix = lax.all_to_all(prefix, CHUNKS, 0, 0, tiled=True)
    out = call(finish_kernel, 1, 4, shape((GROUP, TOK, DV), BF16), 1 << 28)(
        place, prefix, partial, query, norm_gain.reshape(HEADS, DV)
    )
    out = lax.all_to_all(out, "zl", 0, 0, tiled=True)
    return jnp.transpose(out, (1, 0, 2)).reshape(1, TOK, HEADS * DV)


def solution(mesh):
    split = Mesh(mesh.devices.reshape(4, 4, 4, 4, 2), ("y", "zh", "zl", "node", "tp"))
    rows = P("node", CTX, "tp")
    return jax.shard_map(
        local,
        mesh=split,
        in_specs=(rows, rows, rows, rows, P("node", None, None), P(), P("tp")),
        out_specs=rows,
        check_vma=False,
    )
```

time: 939 us -> 170 us (0.18)
  waiting for transfers between devices: 559 us -> 19.8 us
  blocking collectives: 315 us -> 125 us
  between operations: 14.8 us -> 0.07 us
  other arithmetic: 14.8 us -> 0.08 us
  local copies, waits for them, and re-layouts: 15.5 us -> 5.46 us
    psum x1 -> x0, waiting for transfers between devices: 335 us -> none  [spread(): return lax.psum(block, axis)]
    all_gather x2 -> x0, waiting for transfers between devices: 188 us -> none  [entering(): gathered = jax.tree.map(lambda a: lax.all_gather(a, axis), part)]
    psum x1 -> x0, blocking collectives: 140 us -> none  [spread(): return lax.psum(block, axis)]
    all_gather x2 -> x0, blocking collectives: 109 us -> none  [entering(): gathered = jax.tree.map(lambda a: lax.all_gather(a, axis), part)]
    all_to_all x2 -> x3, blocking collectives: 66 us -> 125 us  [the longest x1 83.7 us: local(): lax.all_to_all(packed.reshape(OWNERS, CAP, WIDTH), CTX, 0, 0, tiled=True)]
    all_to_all x2 -> x1, waiting for transfers between devices: 36.3 us -> 19.8 us  [local(): prefix = lax.all_to_all(prefix, CHUNKS, 0, 0, tiled=True)]
  transfers between devices with their start and end apart: 5 -> 1, of which waited for: 4 -> 1; matrix products, arithmetic and copies ran while one was open for 1% -> 0% of each run, Pallas kernels for 0% -> 0%
where the time goes in v1:
time: 170 us; the launch traced here: 168 us
  blocking collectives  125 us (74%)
  waiting for transfers between devices  19.8 us (12%)
  starting transfers between devices  9.34 us (5%)
  Pallas kernels  8.35 us (5%)
  local copies, waits for them, and re-layouts  5.46 us (3%)
    all_to_all x1, blocking collectives, local(): lax.all_to_all(packed.reshape(OWNERS, CAP, WIDTH), CTX, 0, 0, tiled=True)  83.7 us
    all_to_all x1, blocking collectives, local(): maps = lax.all_to_all(maps, CHUNKS, 0, 0, tiled=True)  29.3 us
    all_to_all x1, waiting for transfers between devices, local(): prefix = lax.all_to_all(prefix, CHUNKS, 0, 0, tiled=True)  19.8 us
    all_to_all x1, blocking collectives, local(): out = lax.all_to_all(out, 'zl', 0, 0, tiled=True)  12.1 us
    all_to_all x1, starting transfers between devices, local(): prefix = lax.all_to_all(prefix, CHUNKS, 0, 0, tiled=True)  9.34 us
    pallas_call x1, Pallas kernels, local(): call(chunk_kernel, 2, 2, (shape((OWNERS, 8, DK)), shape((CHUNK, DV)), sha...  5.06 us
    unnamed x14, local copies, waits for them, and re-layouts  4.43 us
  transfers between devices with their start and end apart: 1, of which 1 were waited for; matrix products, arithmetic and copies ran while one was open for 0% of the time, Pallas kernels for 0%

profile of v1, /device:TPU:6, one launch (start us, length us, event | category | flops | bytes accessed | tf_op | source)
XLA Modules:
  0.0 168.2 jit_solution(10756521375577574392)
XLA Ops:
  0.0 0.1 pad_add_fusion.place_ref
  0.1 0.0 copy-start
  0.1 0.9 copy-done
  1.0 0.0 copy-start.1
  1.0 0.9 copy-done.1
  1.9 0.0 copy-start.2
  1.9 0.9 copy-done.2
  2.8 0.0 copy-start.3
  2.8 0.9 copy-done.3
  3.7 0.0 copy-start.4
  3.7 0.8 copy-done.4
  4.5 1.1 shard_map.73
  5.6 0.0 copy-start.5
  5.6 83.7 %all_to_all.20.received_ref = bf16[64,16,640]{2,1,0:T(8,128)(2,1)S(1)} all-to-all(bf16[64,16,640]{2,1,0:T(8,128)(2,1)S(1)} %bitcast.12), channel_id=1, replica_groups=mesh['y'=4,'zh'=4,'zl'=4,'node'=4,'tp'=2] {'y','zh','zl'}, dimensions={0} | all-to-all | bytes 2621440 | tf_op jit(solution)/shard_map/all_to_all | solution.py:197
  89.4 0.0 copy-done.5
  89.4 5.1 %shard_map.74 = (f32[64,8,128]{2,1,0:T(8,128)S(1)}, f32[512,256]{1,0:T(8,128)S(1)}, f32[512,128]{1,0:T(8,128)S(1)}) custom-call(s32[4]{0:T(128)S(1)} %pad_add_fusion.place_ref, s32[8]{0:T(128)S(1)} %copy-done.5, s32[64,64]{1,0:T(8,128)S(1)} %bitcast.18, bf16[64,16,640]{2,1,0:T(8,128)(2,1)S(1)} %all_to_all.20.received_ref), custom_call_target="tpu_custom_call" | custom-call | flops 1073741824 | bytes 1048576 | tf_op jit(solution)/shard_map/pallas_call | solution.py:198
  94.4 0.0 copy-start.6
  94.4 29.3 %all_to_all.21.map_ref = f32[64,8,128]{2,1,0:T(8,128)S(1)} all-to-all(f32[64,8,128]{2,1,0:T(8,128)S(1)} %get-tuple-element.8), channel_id=1, replica_groups=mesh['y'=4,'zh'=4,'zl'=4,'node'=4,'tp'=2] {'node','y','zh'}, dimensions={0} | all-to-all | bytes 524288 | tf_op jit(solution)/shard_map/all_to_all | solution.py:205
  123.8 0.9 shard_map.75
  124.7 9.3 %all-to-all-start.2 = ((f32[64,8,128]{2,1,0:T(8,128)}), f32[64,8,128]{2,1,0:T(8,128)S(1)}, u32[]{:S(2)}, u32[]{:S(2)}) async-start(f32[64,8,128]{2,1,0:T(8,128)} %shard_map.75), calls=%async_computation.2 | async-start | bytes 524288 | tf_op jit(solution)/shard_map/all_to_all | solution.py:207
  134.0 0.0 copy-done.6
  134.1 19.8 %all-to-all-done.2.prefix_ref = f32[64,8,128]{2,1,0:T(8,128)S(1)} async-done(((f32[64,8,128]{2,1,0:T(8,128)}), f32[64,8,128]{2,1,0:T(8,128)S(1)}, u32[]{:S(2)}, u32[]{:S(2)}) %all-to-all-start.2) | async-done | bytes 262176 | tf_op jit(solution)/shard_map/all_to_all | solution.py:207
  153.8 1.3 shard_map.76
  155.1 12.1 %all_to_all.22 = bf16[4,128,256]{2,1,0:T(8,128)(2,1)S(1)} all-to-all(bf16[4,128,256]{2,1,0:T(8,128)(2,1)S(1)} %shard_map.76), channel_id=1, replica_groups=mesh['y'=4,'zh'=4,'zl'=4,'node'=4,'tp'=2] {'zl'}, dimensions={0} | all-to-all | bytes 524288 | tf_op jit(solution)/shard_map/all_to_all | solution.py:211
  167.2 0.2 copy.8
  167.3 0.9 copy.9
  (1 shorter events, 0.0 us)
Async XLA Ops:
  0.1 1.0 copy-start
  1.0 0.9 copy-start.1
  1.9 0.9 copy-start.2
  2.8 0.9 copy-start.3
  3.7 0.8 copy-start.4
  5.6 83.8 %copy-start.5 = (s32[8]{0:T(128)S(1)}, s32[8]{0:T(128)}, u32[]{:S(2)}) copy-start(s32[8]{0:T(128)} %lengths_ref.1) | copy-start | bytes 100
  94.4 39.6 %copy-start.6 = (f32[1024]{0:T(1024)S(1)}, f32[1024]{0:T(1024)}, u32[]{:S(2)}) copy-start(f32[1024]{0:T(1024)} %param.13) | copy-start | bytes 12292
  124.7 29.1 %all-to-all-start.2 = ((f32[64,8,128]{2,1,0:T(8,128)}), f32[64,8,128]{2,1,0:T(8,128)S(1)}, u32[]{:S(2)}, u32[]{:S(2)}) async-start(f32[64,8,128]{2,1,0:T(8,128)} %shard_map.75), calls=%async_computation.2 | async-start | bytes 524288 | tf_op jit(solution)/shard_map/all_to_all | solution.py:207

commit v2 on v1

v2 whole, which is shorter than its diff:
```python
import jax
import jax.numpy as jnp
from jax import lax
from jax.experimental import pallas as pl
from jax.experimental.pallas import tpu as pltpu
from jax.sharding import Mesh, PartitionSpec as P

DK = 128
DV = 256
HEADS = 4
GROUP = 4
TOK = 128
CAP = 16
CHUNK = GROUP * TOK
OWNERS = 64
WIDTH = 3 * DK + DV
EPSILON = 1e-05
CTX = ("y", "zh", "zl")
REGROUP = ("zl", "zh", "y")
CHUNKS = ("node", "y", "zh")
PRECISE = lax.Precision.HIGHEST
F32 = jnp.float32
BF16 = jnp.bfloat16


def iota(shape, dim):
    return lax.broadcasted_iota(jnp.int32, shape, dim)


def dot(a, b, dims=((1,), (0,)), precision=None):
    return lax.dot_general(a, b, (dims, ((), ())), precision=precision, preferred_element_type=F32)


def pack_kernel(
    place_ref, matrix_ref, query_hbm, key_hbm, value_hbm, rate_hbm, out_ref,
    query_ref, key_ref, value_ref, rate_ref, sems,
):
    pairs = ((query_hbm, query_ref), (key_hbm, key_ref), (value_hbm, value_ref), (rate_hbm, rate_ref))
    copies = [pltpu.make_async_copy(a, b, sems.at[i]) for i, (a, b) in enumerate(pairs)]
    for copy in copies:
        copy.start()
    slots = (OWNERS // GROUP) * CAP
    counts = matrix_ref[pl.ds(place_ref[0], 1), :].astype(F32)
    nth = lax.shift_right_logical(iota((slots, OWNERS), 0), 4)
    chunk = (nth & 3) * 4 + lax.shift_right_logical(nth, 2)
    before = iota((slots, OWNERS), 1) < chunk * GROUP
    start = jnp.sum(jnp.where(before, counts, 0.0), axis=1, keepdims=True).astype(jnp.int32)
    wanted = start + (iota((slots, 1), 0) & (CAP - 1))
    pick = (iota((slots, TOK), 1) == wanted).astype(F32).astype(BF16)
    at = 0
    for copy, ref, width in zip(copies, (query_ref, key_ref, value_ref, rate_ref), (DK, DK, DV, DK)):
        copy.wait()
        rows = dot(pick, ref[...]).astype(BF16)
        for head in range(HEADS):
            piece = rows[:, head * width : (head + 1) * width]
            out_ref[head, :, :, at : at + width] = piece.reshape(slots // CAP, CAP, width)
        at += width


def doc_of(lengths_ref, places):
    end = jnp.int32(0)
    doc = jnp.zeros_like(places)
    for d in range(lengths_ref.shape[0]):
        end = end + lengths_ref[d]
        doc = doc + (end <= places).astype(jnp.int32)
    return doc


def unpack(place_ref, matrix_ref, received_ref):
    first = place_ref[1] * GROUP
    matrix = matrix_ref[...].astype(F32).astype(BF16)
    owner = iota((8, OWNERS), 1)
    nth = iota((8, OWNERS), 0)
    one = ((owner == first + nth) & (nth < GROUP)).astype(F32).astype(BF16)
    upto = ((owner >= first) & (owner <= first + nth) & (nth < GROUP)).astype(F32).astype(BF16)
    counts = dot(one, matrix, ((1,), (1,)))
    ends = dot(upto, matrix, ((1,), (1,)))
    earlier = (iota((OWNERS, OWNERS), 0) < iota((OWNERS, OWNERS), 1)).astype(F32).astype(BF16)
    arrive = dot(counts.astype(BF16), earlier)
    slots = OWNERS * CAP
    loader = iota((OWNERS, slots), 0)
    nth = (loader & 3) * 16 + (loader & 12) + lax.shift_right_logical(loader, 4)
    expand = (lax.shift_right_logical(iota((OWNERS, slots), 1), 4) == nth).astype(F32).astype(BF16)
    counts, ends, arrive = [dot(a.astype(BF16), expand) for a in (counts, ends, arrive)]
    slot = (iota((8, slots), 1) & (CAP - 1)).astype(F32)
    inside = (slot < ends) & (slot >= ends - counts)
    target = iota((8, slots), 0).astype(F32) * TOK + arrive + slot - (ends - counts) + 1.0
    target = jnp.sum(jnp.where(inside, target, 0.0), axis=0, keepdims=True).astype(jnp.int32) - 1
    pick = (iota((CHUNK, slots), 0) == target).astype(F32).astype(BF16)
    return dot(pick, received_ref[...].reshape(slots, WIDTH))


def column(row):
    return jnp.transpose(jnp.broadcast_to(row, (DK, DK)))


def decays(rate):
    tril = (iota((TOK, TOK), 0) >= iota((TOK, TOK), 1)).astype(F32)
    parts = []
    for block in range(GROUP):
        log_decay = -jnp.exp(rate[block * TOK : (block + 1) * TOK].astype(F32))
        cumulative = dot(tril, log_decay, precision=PRECISE)
        parts.append((cumulative, cumulative[TOK - 1 :, :]))
    return parts


def doc_at(lengths_ref, place):
    return doc_of(lengths_ref, jnp.full((1, 1), place, jnp.int32))


def maps_kernel(place_ref, lengths_ref, matrix_ref, received_ref, rows_ref, map_ref):
    rows_ref[...] = unpack(place_ref, matrix_ref, received_ref).astype(BF16)
    first = (place_ref[2] * (OWNERS // GROUP) + place_ref[1]) * CHUNK
    parts = decays(rows_ref[:, 2 * DK + DV :])
    after = jnp.zeros((1, DK), F32)
    end_keys = []
    for block in reversed(range(GROUP)):
        cumulative, whole = parts[block]
        key = rows_ref[block * TOK : (block + 1) * TOK, DK : 2 * DK].astype(F32)
        end_keys.insert(0, key * jnp.exp(whole - cumulative + after))
        after = after + whole
    doc_last = doc_at(lengths_ref, first + CHUNK - 1)
    doc_rows = doc_of(lengths_ref, first + iota((CHUNK, DK), 0))
    end_key = jnp.where(doc_rows == doc_last, jnp.concatenate(end_keys, axis=0), 0.0)
    value = rows_ref[:, 2 * DK : 2 * DK + DV].astype(F32)
    state = dot(end_key, value, ((0,), (0,)), PRECISE)
    kept = column(jnp.where(doc_last == doc_at(lengths_ref, first - 1), jnp.exp(after), 0.0))
    half = DK // 2
    map_ref[:, 0, :DV] = state[:half]
    map_ref[:, 0, DV : 2 * DV] = state[half:]
    map_ref[:, 0, 2 * DV :] = jnp.where(iota((half, DK), 1) < half, kept[:half], kept[half:])


def block_kernel(place_ref, lengths_ref, rows_ref, partial_ref, query_out_ref):
    first = (place_ref[2] * (OWNERS // GROUP) + place_ref[1]) * CHUNK
    state = None
    passed = jnp.zeros((1, DK), F32)
    chunk_before = doc_at(lengths_ref, first - 1)
    for block, (cumulative, whole) in enumerate(decays(rows_ref[:, 2 * DK + DV :])):
        span = slice(block * TOK, (block + 1) * TOK)
        query = rows_ref[span, :DK].astype(F32)
        key = rows_ref[span, DK : 2 * DK].astype(F32)
        value = rows_ref[span, 2 * DK : 2 * DK + DV].astype(F32)
        start = first + block * TOK
        doc_rows = doc_of(lengths_ref, start + iota((TOK, DK), 0))
        doc_columns = doc_of(lengths_ref, start + iota((TOK, TOK), 1))
        doc_before = doc_at(lengths_ref, start - 1)
        doc_last = doc_at(lengths_ref, start + TOK - 1)
        half = 0.5 * whole
        scores = dot(
            query * jnp.exp(cumulative - half),
            key * jnp.exp(half - cumulative),
            ((1,), (1,)),
            PRECISE,
        )
        allowed = (iota((TOK, TOK), 0) >= iota((TOK, TOK), 1)) & (doc_rows == doc_columns)
        out = dot(jnp.where(allowed, scores, 0.0), value, precision=PRECISE)
        if block > 0:
            kept = jnp.where(doc_rows == doc_before, query * jnp.exp(cumulative), 0.0)
            out = out + dot(kept, state, precision=PRECISE)
        partial_ref[span, :] = out
        query_out_ref[span, :] = jnp.where(
            doc_rows == chunk_before, query * jnp.exp(cumulative + passed), 0.0
        )
        if block < GROUP - 1:
            end_key = jnp.where(doc_rows == doc_last, key * jnp.exp(whole - cumulative), 0.0)
            fresh = dot(end_key, value, ((0,), (0,)), PRECISE)
            if block == 0:
                state = fresh
            else:
                kept = column(jnp.where(doc_last == doc_before, jnp.exp(whole), 0.0))
                state = jnp.concatenate([kept, kept], axis=1) * state + fresh
        passed = passed + whole


def scan_kernel(map_ref, prefix_ref):
    low = iota((1, DK), 1) < DK // 2

    def step(chunk, state):
        prefix_ref[chunk] = state
        here = map_ref[chunk]
        kept = here[:, 2 * DV :]
        other = pltpu.roll(kept, DK // 2, 1)
        one, two = jnp.where(low, kept, other), jnp.where(low, other, kept)
        return jnp.concatenate([one, one, two, two], axis=1) * state + here[:, : 2 * DV]

    lax.fori_loop(0, map_ref.shape[0], step, jnp.zeros((1, 2 * DV), F32), unroll=True)


def finish_kernel(place_ref, prefix_ref, partial_ref, query_ref, gain_ref, out_ref):
    state = jnp.concatenate([prefix_ref[:, 0, :DV], prefix_ref[:, 0, DV:]], axis=0)
    gain = gain_ref[pl.ds(place_ref[3], 1), :]
    for block in range(GROUP):
        span = slice(block * TOK, (block + 1) * TOK)
        mixed = partial_ref[span, :] + dot(query_ref[span, :], state, precision=PRECISE)
        scale = lax.rsqrt(jnp.mean(mixed * mixed, axis=1, keepdims=True) + EPSILON)
        out_ref[block] = (mixed * scale * gain).astype(BF16)


SMEM = pl.BlockSpec(memory_space=pltpu.SMEM)
VMEM = pl.BlockSpec(memory_space=pltpu.VMEM)
HBM = pl.BlockSpec(memory_space=pltpu.HBM)


def call(kernel, specs, outs, cost=0, scratch=()):
    return pl.pallas_call(
        kernel,
        out_shape=outs,
        in_specs=specs,
        out_specs=jax.tree.map(lambda _: VMEM, outs),
        scratch_shapes=scratch,
        compiler_params=pltpu.CompilerParams(vmem_limit_bytes=32 << 20),
        cost_estimate=pl.CostEstimate(flops=cost, bytes_accessed=1 << 20, transcendentals=0),
    )


def shape(dims, dtype=F32):
    return jax.ShapeDtypeStruct(dims, dtype)


def local(queries, key_vectors, value_vectors, decay_log, assignment, doc_lengths, norm_gain):
    own = lax.axis_index(CTX)
    place = jnp.stack([own, own // GROUP, lax.axis_index("node"), own % GROUP]).astype(jnp.int32)
    matrix = assignment[0]
    streams = (queries[0], key_vectors[0], value_vectors[0], decay_log[0])
    packed = call(
        pack_kernel,
        [SMEM, VMEM] + [HBM] * 4,
        shape((HEADS, OWNERS // GROUP, CAP, WIDTH), BF16),
        1 << 28,
        [pltpu.VMEM(a.shape, BF16) for a in streams] + [pltpu.SemaphoreType.DMA((4,))],
    )(place, matrix, *streams)
    received = lax.all_to_all(packed.reshape(OWNERS, CAP, WIDTH), REGROUP, 0, 0, tiled=True)
    rows, maps = call(
        maps_kernel,
        [SMEM, SMEM, VMEM, VMEM],
        (shape((CHUNK, WIDTH), BF16), shape((OWNERS, 1, 2 * DV + DK))),
        1 << 29,
    )(place, doc_lengths, matrix, received)
    maps = lax.all_to_all(maps, CHUNKS, 0, 0, tiled=True)
    partial, query = call(
        block_kernel,
        [SMEM, SMEM, VMEM],
        (shape((CHUNK, DV)), shape((CHUNK, DK))),
        1 << 30,
    )(place, doc_lengths, rows)
    prefix = call(scan_kernel, [VMEM], shape((OWNERS, 1, 2 * DV)), 1 << 24)(maps)
    prefix = lax.all_to_all(prefix, CHUNKS, 0, 0, tiled=True)
    out = call(finish_kernel, [SMEM] + [VMEM] * 4, shape((GROUP, TOK, DV), BF16), 1 << 28)(
        place, prefix, partial, query, norm_gain.reshape(HEADS, DV)
    )
    out = lax.all_to_all(out, "zl", 0, 0, tiled=True)
    return jnp.transpose(out, (1, 0, 2)).reshape(1, TOK, HEADS * DV)


def solution(mesh):
    split = Mesh(mesh.devices.reshape(4, 4, 4, 4, 2), ("y", "zh", "zl", "node", "tp"))
    rows = P("node", CTX, "tp")
    return jax.shard_map(
        local,
        mesh=split,
        in_specs=(rows, rows, rows, rows, P("node", None, None), P(), P("tp")),
        out_specs=rows,
        check_vma=False,
    )
```

time: 170 us -> 161 us (0.947)
  waiting for transfers between devices: 19.8 us -> 13.7 us
  starting transfers between devices: 9.34 us -> 6.69 us
  Pallas kernels: 8.35 us -> 10.8 us
  blocking collectives: 125 us -> 123 us
    all_to_all x1, waiting for transfers between devices: 19.8 us -> 13.7 us  [local(): prefix = lax.all_to_all(prefix, CHUNKS, 0, 0, tiled=True)]
    all_to_all x1, starting transfers between devices: 9.34 us -> 6.69 us  [local(): prefix = lax.all_to_all(prefix, CHUNKS, 0, 0, tiled=True)]
    pallas_call x4 -> x5, Pallas kernels: 8.35 us -> 10.8 us  [the longest x1 3.49 us: local(): call(maps_kernel, [SMEM, SMEM, VMEM, VMEM], (shape((CHUNK, WIDTH), BF16),...]
    all_to_all x1, blocking collectives: 83.7 us -> 81.4 us  [local(): lax.all_to_all(packed.reshape(OWNERS, CAP, WIDTH), REGROUP, 0, 0, tiled=T...]
  transfers between devices with their start and end apart: 1 -> 1, of which waited for: 1 -> 1; matrix products, arithmetic and copies ran while one was open for 0% -> 0% of each run, Pallas kernels for 0% -> 2%
where the time goes in v2:
time: 161 us; the launch traced here: 160 us
  blocking collectives  123 us (76%)
  waiting for transfers between devices  13.7 us (9%)
  Pallas kernels  10.8 us (7%)
  starting transfers between devices  6.69 us (4%)
  local copies, waits for them, and re-layouts  5.46 us (3%)
    all_to_all x1, blocking collectives, local(): lax.all_to_all(packed.reshape(OWNERS, CAP, WIDTH), REGROUP, 0, 0, tiled=T...  81.4 us
    all_to_all x1, blocking collectives, local(): maps = lax.all_to_all(maps, CHUNKS, 0, 0, tiled=True)  30.3 us
    all_to_all x1, waiting for transfers between devices, local(): prefix = lax.all_to_all(prefix, CHUNKS, 0, 0, tiled=True)  13.7 us
    all_to_all x1, blocking collectives, local(): out = lax.all_to_all(out, 'zl', 0, 0, tiled=True)  11.2 us
    all_to_all x1, starting transfers between devices, local(): prefix = lax.all_to_all(prefix, CHUNKS, 0, 0, tiled=True)  6.69 us
    unnamed x14, local copies, waits for them, and re-layouts  4.43 us
    pallas_call x1, Pallas kernels, local(): call(maps_kernel, [SMEM, SMEM, VMEM, VMEM], (shape((CHUNK, WIDTH), BF16),...  3.49 us
  transfers between devices with their start and end apart: 1, of which 1 were waited for; matrix products, arithmetic and copies ran while one was open for 0% of the time, Pallas kernels for 2%

profile of v2, /device:TPU:6, one launch (start us, length us, event | category | flops | bytes accessed | tf_op | source)
XLA Modules:
  0.0 159.7 jit_solution(4738455744403503584)
XLA Ops:
  0.0 0.1 pad_add_fusion.place_ref
  0.1 0.0 copy-start
  0.1 0.9 copy-done
  1.0 0.0 copy-start.1
  1.0 0.9 copy-done.1
  1.9 0.0 copy-start.2
  1.9 0.9 copy-done.2
  2.8 0.0 copy-start.3
  2.8 0.9 copy-done.3
  3.7 0.0 copy-start.4
  3.7 0.8 copy-done.4
  4.5 2.2 %shard_map.73 = bf16[4,16,16,640]{3,2,1,0:T(8,128)(2,1)S(1)} custom-call(s32[4]{0:T(128)S(1)} %pad_add_fusion.place_ref, s32[64,64]{1,0:T(8,128)S(1)} %bitcast.17, bf16[128,512]{1,0:T(8,128)(2,1)S(1)} %bitcast.14, bf16[128,512]{1,0:T(8,128)(2,1)S(1)} %bitcast.15, bf16[128,1024]{1,0:T(8,128)(2,1)S(1)} %bitcast.13, bf16[128,512]{1,0:T(8,128)(2,1)S(1)} %bitcast.16), custom_call_target="tpu_custom_call" | custom-call | flops 268435456 | bytes 1048576 | tf_op jit(solution)/shard_map/pallas_call | solution.py:226
  6.7 0.0 copy-start.5
  6.7 81.4 %all_to_all.20.received_ref = bf16[64,16,640]{2,1,0:T(8,128)(2,1)S(1)} all-to-all(bf16[64,16,640]{2,1,0:T(8,128)(2,1)S(1)} %bitcast.12), channel_id=1, replica_groups=mesh['y'=4,'zh'=4,'zl'=4,'node'=4,'tp'=2] {'zl','zh','y'}, dimensions={0} | all-to-all | bytes 2621440 | tf_op jit(solution)/shard_map/all_to_all | solution.py:233
  88.1 0.0 copy-done.5
  88.1 0.0 copy-start.6
  88.1 3.5 %shard_map.74 = (bf16[512,640]{1,0:T(8,128)(2,1)S(1)}, f32[64,1,640]{2,1,0:T(1,128)S(1)}) custom-call(s32[4]{0:T(128)S(1)} %pad_add_fusion.place_ref, s32[8]{0:T(128)S(1)} %copy-done.5, s32[64,64]{1,0:T(8,128)S(1)} %bitcast.18, bf16[64,16,640]{2,1,0:T(8,128)(2,1)S(1)} %all_to_all.20.received_ref), custom_call_target="tpu_custom_call" | custom-call | flops 536870912 | bytes 1048576 | tf_op jit(solution)/shard_map/pallas_call | solution.py:234
  91.6 30.3 %all_to_all.21.map_ref = f32[64,1,640]{2,1,0:T(1,128)S(1)} all-to-all(f32[64,1,640]{2,1,0:T(1,128)S(1)} %get-tuple-element.9), channel_id=1, replica_groups=mesh['y'=4,'zh'=4,'zl'=4,'node'=4,'tp'=2] {'node','y','zh'}, dimensions={0} | all-to-all | bytes 327680 | tf_op jit(solution)/shard_map/all_to_all | solution.py:240
  121.9 0.9 shard_map.75
  122.7 6.7 %all-to-all-start.2 = ((f32[64,1,512]{2,1,0:T(1,128)}), f32[64,1,512]{2,1,0:T(1,128)S(1)}, u32[]{:S(2)}, u32[]{:S(2)}) async-start(f32[64,1,512]{2,1,0:T(1,128)} %shard_map.75), calls=%async_computation.2 | async-start | bytes 262144 | tf_op jit(solution)/shard_map/all_to_all | solution.py:248
  129.4 0.0 copy-done.6
  129.4 3.1 %shard_map.76 = (f32[512,256]{1,0:T(8,128)S(1)}, f32[512,128]{1,0:T(8,128)S(1)}) custom-call(s32[4]{0:T(128)S(1)} %pad_add_fusion.place_ref, s32[8]{0:T(128)S(1)} %copy-done.5, bf16[512,640]{1,0:T(8,128)(2,1)S(1)} %get-tuple-element.10.rows_ref), custom_call_target="tpu_custom_call" | custom-call | flops 1073741824 | bytes 1048576 | tf_op jit(solution)/shard_map/pallas_call | solution.py:241
  132.5 13.7 %all-to-all-done.2.prefix_ref = f32[64,1,512]{2,1,0:T(1,128)S(1)} async-done(((f32[64,1,512]{2,1,0:T(1,128)}), f32[64,1,512]{2,1,0:T(1,128)S(1)}, u32[]{:S(2)}, u32[]{:S(2)}) %all-to-all-start.2) | async-done | bytes 131104 | tf_op jit(solution)/shard_map/all_to_all | solution.py:248
  146.3 1.2 shard_map.77
  147.5 11.2 %all_to_all.22 = bf16[4,128,256]{2,1,0:T(8,128)(2,1)S(1)} all-to-all(bf16[4,128,256]{2,1,0:T(8,128)(2,1)S(1)} %shard_map.77), channel_id=1, replica_groups=mesh['y'=4,'zh'=4,'zl'=4,'node'=4,'tp'=2] {'zl'}, dimensions={0} | all-to-all | bytes 524288 | tf_op jit(solution)/shard_map/all_to_all | solution.py:252
  158.7 0.2 copy.8
  158.9 0.9 copy.9
  (1 shorter events, 0.0 us)
Async XLA Ops:
  0.1 1.0 copy-start
  1.0 0.9 copy-start.1
  1.9 0.9 copy-start.2
  2.8 0.9 copy-start.3
  3.7 0.8 copy-start.4
  6.7 81.4 %copy-start.5 = (s32[8]{0:T(128)S(1)}, s32[8]{0:T(128)}, u32[]{:S(2)}) copy-start(s32[8]{0:T(128)} %lengths_ref.3) | copy-start | bytes 100
  88.1 41.3 %copy-start.6 = (f32[1024]{0:T(1024)S(1)}, f32[1024]{0:T(1024)}, u32[]{:S(2)}) copy-start(f32[1024]{0:T(1024)} %param.13) | copy-start | bytes 12292
  122.7 23.5 %all-to-all-start.2 = ((f32[64,1,512]{2,1,0:T(1,128)}), f32[64,1,512]{2,1,0:T(1,128)S(1)}, u32[]{:S(2)}, u32[]{:S(2)}) async-start(f32[64,1,512]{2,1,0:T(1,128)} %shard_map.75), calls=%async_computation.2 | async-start | bytes 262144 | tf_op jit(solution)/shard_map/all_to_all | solution.py:248

commit v3 on v2

v3 whole, which is shorter than its diff:
```python
import jax
import jax.numpy as jnp
from jax import lax
from jax.experimental import pallas as pl
from jax.experimental.pallas import tpu as pltpu
from jax.sharding import Mesh, PartitionSpec as P

DK = 128
DV = 256
HEADS = 4
GROUP = 4
TOK = 128
CAP = 16
CHUNK = GROUP * TOK
OWNERS = 64
LATE = 2 * DK + DV
WIDTH = LATE + DK
EPSILON = 1e-05
CTX = ("y", "zh", "zl")
REGROUP = ("zl", "zh", "y")
CHUNKS = ("node", "y", "zh")
PRECISE = lax.Precision.HIGHEST
F32 = jnp.float32
BF16 = jnp.bfloat16


def iota(shape, dim):
    return lax.broadcasted_iota(jnp.int32, shape, dim)


def dot(a, b, dims=((1,), (0,)), precision=None):
    return lax.dot_general(a, b, (dims, ((), ())), precision=precision, preferred_element_type=F32)


def split(a):
    high = a.astype(BF16)
    rest = a - high.astype(F32)
    middle = rest.astype(BF16)
    return high, middle, (rest - middle.astype(F32)).astype(BF16)


def dot_left(a, b, dims=((1,), (0,))):
    high, middle, low = split(a)
    return dot(high, b, dims) + (dot(middle, b, dims) + dot(low, b, dims))


def pack_kernel(
    matrix_hbm, query_hbm, key_hbm, value_hbm, rate_hbm, out_ref,
    matrix_ref, query_ref, key_ref, value_ref, rate_ref, sems,
):
    sources = (matrix_hbm, key_hbm, rate_hbm, value_hbm, query_hbm)
    targets = (matrix_ref, key_ref, rate_ref, value_ref, query_ref)
    copies = [pltpu.make_async_copy(a, b, sems.at[i]) for i, (a, b) in enumerate(zip(sources, targets))]
    for copy in copies:
        copy.start()
    copies[0].wait()
    slots = (OWNERS // GROUP) * CAP
    counts = matrix_ref[pl.ds(lax.axis_index(CTX), 1), :].astype(F32)
    nth = lax.shift_right_logical(iota((slots, OWNERS), 0), 4)
    chunk = (nth & 3) * 4 + lax.shift_right_logical(nth, 2)
    before = iota((slots, OWNERS), 1) < chunk * GROUP
    start = jnp.sum(jnp.where(before, counts, 0.0), axis=1, keepdims=True).astype(jnp.int32)
    wanted = start + (iota((slots, 1), 0) & (CAP - 1))
    pick = (iota((slots, TOK), 1) == wanted).astype(F32).astype(BF16)
    at = 0
    for copy, ref, width in zip(copies[1:], targets[1:], (DK, DK, DV, DK)):
        copy.wait()
        rows = dot(pick, ref[...]).astype(BF16)
        for head in range(HEADS):
            piece = rows[:, head * width : (head + 1) * width]
            out_ref[head, :, :, at : at + width] = piece.reshape(slots // CAP, CAP, width)
        at += width


def chunk_in_group():
    return lax.axis_index("y") * 4 + lax.axis_index("zh")


def chunk_start():
    return (lax.axis_index("node") * (OWNERS // GROUP) + chunk_in_group()) * CHUNK


def doc_of(lengths_ref, places):
    end = jnp.int32(0)
    doc = jnp.zeros_like(places)
    for d in range(lengths_ref.shape[0]):
        end = end + lengths_ref[d]
        doc = doc + (end <= places).astype(jnp.int32)
    return doc


def slot_targets(matrix_ref):
    first = chunk_in_group() * GROUP
    matrix = matrix_ref[...].astype(F32).astype(BF16)
    owner = iota((8, OWNERS), 1)
    nth = iota((8, OWNERS), 0)
    one = ((owner == first + nth) & (nth < GROUP)).astype(F32).astype(BF16)
    upto = ((owner >= first) & (owner <= first + nth) & (nth < GROUP)).astype(F32).astype(BF16)
    counts = dot(one, matrix, ((1,), (1,)))
    ends = dot(upto, matrix, ((1,), (1,)))
    earlier = (iota((OWNERS, OWNERS), 0) < iota((OWNERS, OWNERS), 1)).astype(F32).astype(BF16)
    arrive = dot(counts.astype(BF16), earlier)
    slots = OWNERS * CAP
    loader = iota((OWNERS, slots), 0)
    nth = (loader & 3) * 16 + (loader & 12) + lax.shift_right_logical(loader, 4)
    expand = (lax.shift_right_logical(iota((OWNERS, slots), 1), 4) == nth).astype(F32).astype(BF16)
    wide = dot(jnp.concatenate([counts, ends, arrive], axis=0).astype(BF16), expand)
    counts, ends, arrive = wide[:8], wide[8:16], wide[16:]
    slot = (iota((8, slots), 1) & (CAP - 1)).astype(F32)
    inside = (slot < ends) & (slot >= ends - counts)
    target = iota((8, slots), 0).astype(F32) * TOK + arrive + slot - (ends - counts) + 1.0
    return jnp.sum(jnp.where(inside, target, 0.0), axis=0, keepdims=True).astype(jnp.int32) - 1


def unpack(targets, received):
    pick = (iota((CHUNK, OWNERS * CAP), 0) == targets).astype(F32).astype(BF16)
    return dot(pick, received.reshape(OWNERS * CAP, received.shape[2])).astype(BF16)


def column(row):
    return jnp.transpose(jnp.broadcast_to(row, (DK, DK)))


def decays(rate):
    rate = jnp.concatenate([rate[i * TOK : (i + 1) * TOK] for i in range(GROUP)], axis=1)
    tril = (iota((TOK, TOK), 0) >= iota((TOK, TOK), 1)).astype(F32).astype(BF16)
    high, middle, low = split(-jnp.exp(rate.astype(F32)))
    cumulative = dot(tril, high) + (dot(tril, middle) + dot(tril, low))
    parts = [cumulative[:, i * DK : (i + 1) * DK] for i in range(GROUP)]
    return [(part, part[TOK - 1 :, :]) for part in parts]


def doc_at(lengths_ref, place):
    return doc_of(lengths_ref, jnp.full((1, 1), place, jnp.int32))


def maps_kernel(lengths_ref, matrix_ref, received_ref, rows_ref, targets_ref, map_ref):
    targets = slot_targets(matrix_ref)
    targets_ref[...] = targets
    rows_ref[...] = unpack(targets, received_ref[:, :, :LATE])
    first = chunk_start()
    parts = decays(rows_ref[:, DK : 2 * DK])
    after = jnp.zeros((1, DK), F32)
    end_keys = []
    for block in reversed(range(GROUP)):
        cumulative, whole = parts[block]
        key = rows_ref[block * TOK : (block + 1) * TOK, :DK].astype(F32)
        end_keys.insert(0, key * jnp.exp(whole - cumulative + after))
        after = after + whole
    doc_last = doc_at(lengths_ref, first + CHUNK - 1)
    doc_rows = doc_of(lengths_ref, first + iota((CHUNK, DK), 0))
    end_key = jnp.where(doc_rows == doc_last, jnp.concatenate(end_keys, axis=0), 0.0)
    state = dot_left(end_key, rows_ref[:, 2 * DK :], ((0,), (0,)))
    kept = column(jnp.where(doc_last == doc_at(lengths_ref, first - 1), jnp.exp(after), 0.0))
    half = DK // 2
    map_ref[:, 0, :DV] = state[:half]
    map_ref[:, 0, DV : 2 * DV] = state[half:]
    map_ref[:, 0, 2 * DV :] = jnp.where(iota((half, DK), 1) < half, kept[:half], kept[half:])


def block_kernel(lengths_ref, targets_ref, received_ref, rows_ref, partial_ref, query_out_ref):
    first = chunk_start()
    queries = unpack(targets_ref[...], received_ref[:, :, LATE:])
    state = None
    passed = jnp.zeros((1, DK), F32)
    chunk_before = doc_at(lengths_ref, first - 1)
    for block, (cumulative, whole) in enumerate(decays(rows_ref[:, DK : 2 * DK])):
        span = slice(block * TOK, (block + 1) * TOK)
        query = queries[span].astype(F32)
        key = rows_ref[span, :DK].astype(F32)
        value = rows_ref[span, 2 * DK :]
        start = first + block * TOK
        doc_rows = doc_of(lengths_ref, start + iota((TOK, DK), 0))
        doc_columns = doc_of(lengths_ref, start + iota((TOK, TOK), 1))
        doc_before = doc_at(lengths_ref, start - 1)
        doc_last = doc_at(lengths_ref, start + TOK - 1)
        half = 0.5 * whole
        scores = dot(
            query * jnp.exp(cumulative - half),
            key * jnp.exp(half - cumulative),
            ((1,), (1,)),
            PRECISE,
        )
        allowed = (iota((TOK, TOK), 0) >= iota((TOK, TOK), 1)) & (doc_rows == doc_columns)
        out = dot_left(jnp.where(allowed, scores, 0.0), value)
        if block > 0:
            kept = jnp.where(doc_rows == doc_before, query * jnp.exp(cumulative), 0.0)
            out = out + dot(kept, state, precision=PRECISE)
        partial_ref[span, :] = out
        query_out_ref[span, :] = jnp.where(
            doc_rows == chunk_before, query * jnp.exp(cumulative + passed), 0.0
        )
        if block < GROUP - 1:
            end_key = jnp.where(doc_rows == doc_last, key * jnp.exp(whole - cumulative), 0.0)
            fresh = dot_left(end_key, value, ((0,), (0,)))
            if block == 0:
                state = fresh
            else:
                kept = column(jnp.where(doc_last == doc_before, jnp.exp(whole), 0.0))
                state = jnp.concatenate([kept, kept], axis=1) * state + fresh
        passed = passed + whole


def scan_kernel(map_ref, prefix_ref):
    low = iota((1, DK), 1) < DK // 2

    def step(chunk, state):
        prefix_ref[chunk] = state
        here = map_ref[chunk]
        kept = here[:, 2 * DV :]
        other = pltpu.roll(kept, DK // 2, 1)
        one, two = jnp.where(low, kept, other), jnp.where(low, other, kept)
        return jnp.concatenate([one, one, two, two], axis=1) * state + here[:, : 2 * DV]

    lax.fori_loop(0, map_ref.shape[0], step, jnp.zeros((1, 2 * DV), F32), unroll=True)


def finish_kernel(prefix_ref, partial_ref, query_ref, gain_ref, out_ref):
    state = jnp.concatenate([prefix_ref[:, 0, :DV], prefix_ref[:, 0, DV:]], axis=0)
    gain = gain_ref[pl.ds(lax.axis_index("zl"), 1), :]
    for block in range(GROUP):
        span = slice(block * TOK, (block + 1) * TOK)
        mixed = partial_ref[span, :] + dot(query_ref[span, :], state, precision=PRECISE)
        scale = lax.rsqrt(jnp.mean(mixed * mixed, axis=1, keepdims=True) + EPSILON)
        out_ref[block] = (mixed * scale * gain).astype(BF16)


SMEM = pl.BlockSpec(memory_space=pltpu.SMEM)
VMEM = pl.BlockSpec(memory_space=pltpu.VMEM)
HBM = pl.BlockSpec(memory_space=pltpu.HBM)


def call(kernel, specs, outs, cost=0, scratch=(), limit=32 << 20):
    return pl.pallas_call(
        kernel,
        out_shape=outs,
        in_specs=specs,
        out_specs=jax.tree.map(lambda _: VMEM, outs),
        scratch_shapes=scratch,
        compiler_params=pltpu.CompilerParams(vmem_limit_bytes=limit),
        cost_estimate=pl.CostEstimate(flops=cost, bytes_accessed=1 << 20, transcendentals=0),
    )


def shape(dims, dtype=F32):
    return jax.ShapeDtypeStruct(dims, dtype)


def local(queries, key_vectors, value_vectors, decay_log, assignment, doc_lengths, norm_gain):
    matrix = assignment[0]
    streams = (matrix, queries[0], key_vectors[0], value_vectors[0], decay_log[0])
    packed = call(
        pack_kernel,
        [HBM] * 5,
        shape((HEADS, OWNERS // GROUP, CAP, WIDTH), BF16),
        1 << 28,
        [pltpu.VMEM(a.shape, a.dtype) for a in streams] + [pltpu.SemaphoreType.DMA((5,))],
        65500000,
    )(*streams)
    received = lax.all_to_all(packed.reshape(OWNERS, CAP, WIDTH), REGROUP, 0, 0, tiled=True)
    rows, targets, maps = call(
        maps_kernel,
        [SMEM, VMEM, VMEM],
        (
            shape((CHUNK, LATE), BF16),
            shape((1, OWNERS * CAP), jnp.int32),
            shape((OWNERS, 1, 2 * DV + DK)),
        ),
        1 << 29,
    )(doc_lengths, matrix, received)
    maps = lax.all_to_all(maps, CHUNKS, 0, 0, tiled=True)
    partial, query = call(
        block_kernel,
        [SMEM, VMEM, VMEM, VMEM],
        (shape((CHUNK, DV)), shape((CHUNK, DK))),
        1 << 30,
    )(doc_lengths, targets, received, rows)
    prefix = call(scan_kernel, [VMEM], shape((OWNERS, 1, 2 * DV)), 1 << 24)(maps)
    prefix = lax.all_to_all(prefix, CHUNKS, 0, 0, tiled=True)
    out = call(finish_kernel, [VMEM] * 4, shape((GROUP, TOK, DV), BF16), 1 << 28)(
        prefix, partial, query, norm_gain.reshape(HEADS, DV)
    )
    out = lax.all_to_all(out, "zl", 0, 0, tiled=True)
    return jnp.transpose(out, (1, 0, 2)).reshape(1, TOK, HEADS * DV)


def solution(mesh):
    split = Mesh(mesh.devices.reshape(4, 4, 4, 4, 2), ("y", "zh", "zl", "node", "tp"))
    rows = P("node", CTX, "tp")
    return jax.shard_map(
        local,
        mesh=split,
        in_specs=(rows, rows, rows, rows, P("node", None, None), P(), P("tp")),
        out_specs=rows,
        check_vma=False,
    )
```

time: 161 us -> 156 us (0.969)
  local copies, waits for them, and re-layouts: 5.46 us -> 1.05 us
    unnamed x14 -> x6, local copies, waits for them, and re-layouts: 4.43 us -> 0.02 us
where the time goes in v3:
time: 156 us; the launch traced here: 155 us
  blocking collectives  123 us (79%)
  waiting for transfers between devices  13.6 us (9%)
  Pallas kernels  10.2 us (7%)
  starting transfers between devices  6.69 us (4%)
    all_to_all x1, blocking collectives, local(): lax.all_to_all(packed.reshape(OWNERS, CAP, WIDTH), REGROUP, 0, 0, tiled=T...  81.6 us
    all_to_all x1, blocking collectives, local(): maps = lax.all_to_all(maps, CHUNKS, 0, 0, tiled=True)  30.3 us
    all_to_all x1, waiting for transfers between devices, local(): prefix = lax.all_to_all(prefix, CHUNKS, 0, 0, tiled=True)  13.6 us
    all_to_all x1, blocking collectives, local(): out = lax.all_to_all(out, 'zl', 0, 0, tiled=True)  11.2 us
    all_to_all x1, starting transfers between devices, local(): prefix = lax.all_to_all(prefix, CHUNKS, 0, 0, tiled=True)  6.69 us
    pallas_call x1, Pallas kernels, local(): call(block_kernel, [SMEM, VMEM, VMEM, VMEM], (shape((CHUNK, DV)), shape((...  3.25 us
  transfers between devices with their start and end apart: 1, of which 1 were waited for; matrix products, arithmetic and copies ran while one was open for 0% of the time, Pallas kernels for 2%

profile of v3, /device:TPU:6, one launch (start us, length us, event | category | flops | bytes accessed | tf_op | source)
XLA Modules:
  0.0 154.7 jit_solution(13442170306448513550)
XLA Ops:
  0.0 3.0 %shard_map.73 = bf16[4,16,16,640]{3,2,1,0:T(8,128)(2,1)} custom-call(s32[64,64]{1,0:T(8,128)} %bitcast.8, bf16[128,512]{1,0:T(8,128)(2,1)} %bitcast.14, bf16[128,512]{1,0:T(8,128)(2,1)} %bitcast.15, bf16[128,1024]{1,0:T(8,128)(2,1)} %bitcast.13, bf16[128,512]{1,0:T(8,128)(2,1)} %bitcast.16), custom_call_target="tpu_custom_call" | custom-call | flops 268435456 | bytes 1048576 | tf_op jit(solution)/shard_map/pallas_call | solution.py:252
  3.0 0.0 copy-start
  3.0 0.0 copy-start.1
  3.0 81.6 %all_to_all.20.received_ref = bf16[64,16,640]{2,1,0:T(8,128)(2,1)S(1)} all-to-all(bf16[64,16,640]{2,1,0:T(8,128)(2,1)} %bitcast.10), channel_id=1, replica_groups=mesh['y'=4,'zh'=4,'zl'=4,'node'=4,'tp'=2] {'zl','zh','y'}, dimensions={0} | all-to-all | bytes 2621440 | tf_op jit(solution)/shard_map/all_to_all | solution.py:260
  84.6 0.0 copy-done
  84.6 0.0 copy-done.1
  84.6 0.0 copy-start.2
  84.6 2.5 %shard_map.74 = (bf16[512,512]{1,0:T(8,128)(2,1)S(1)}, s32[1,1024]{1,0:T(1,128)S(1)}, f32[64,1,640]{2,1,0:T(1,128)S(1)}) custom-call(s32[8]{0:T(128)S(1)} %copy-done.1, s32[64,64]{1,0:T(8,128)S(1)} %bitcast.9, bf16[64,16,640]{2,1,0:T(8,128)(2,1)S(1)} %all_to_all.20.received_ref), custom_call_target="tpu_custom_call" | custom-call | flops 536870912 | bytes 1048576 | tf_op jit(solution)/shard_map/pallas_call | solution.py:261
  87.1 30.3 %all_to_all.21.map_ref = f32[64,1,640]{2,1,0:T(1,128)S(1)} all-to-all(f32[64,1,640]{2,1,0:T(1,128)S(1)} %get-tuple-element.10), channel_id=1, replica_groups=mesh['y'=4,'zh'=4,'zl'=4,'node'=4,'tp'=2] {'node','y','zh'}, dimensions={0} | all-to-all | bytes 327680 | tf_op jit(solution)/shard_map/all_to_all | solution.py:271
  117.3 0.9 shard_map.75
  118.2 6.7 %all-to-all-start.2 = ((f32[64,1,512]{2,1,0:T(1,128)}), f32[64,1,512]{2,1,0:T(1,128)S(1)}, u32[]{:S(2)}, u32[]{:S(2)}) async-start(f32[64,1,512]{2,1,0:T(1,128)} %shard_map.75), calls=%async_computation.2 | async-start | bytes 262144 | tf_op jit(solution)/shard_map/all_to_all | solution.py:279
  124.9 0.0 copy-done.2
  124.9 3.3 %shard_map.76 = (f32[512,256]{1,0:T(8,128)S(1)}, f32[512,128]{1,0:T(8,128)S(1)}) custom-call(s32[8]{0:T(128)S(1)} %copy-done.1, s32[1,1024]{1,0:T(1,128)S(1)} %get-tuple-element.11.targets_ref, bf16[64,16,640]{2,1,0:T(8,128)(2,1)S(1)} %all_to_all.20.received_ref, bf16[512,512]{1,0:T(8,128)(2,1)S(1)} %get-tuple-element.12.rows_ref), custom_call_target="tpu_custom_call" | custom-call | flops 1073741824 | bytes 1048576 | tf_op jit(solution)/shard_map/pallas_call | solution.py:272
  128.2 13.6 %all-to-all-done.2.prefix_ref = f32[64,1,512]{2,1,0:T(1,128)S(1)} async-done(((f32[64,1,512]{2,1,0:T(1,128)}), f32[64,1,512]{2,1,0:T(1,128)S(1)}, u32[]{:S(2)}, u32[]{:S(2)}) %all-to-all-start.2) | async-done | bytes 131104 | tf_op jit(solution)/shard_map/all_to_all | solution.py:279
  141.8 0.7 shard_map.77
  142.4 11.2 %all_to_all.22 = bf16[4,128,256]{2,1,0:T(8,128)(2,1)S(1)} all-to-all(bf16[4,128,256]{2,1,0:T(8,128)(2,1)S(1)} %shard_map.77), channel_id=1, replica_groups=mesh['y'=4,'zh'=4,'zl'=4,'node'=4,'tp'=2] {'zl'}, dimensions={0} | all-to-all | bytes 524288 | tf_op jit(solution)/shard_map/all_to_all | solution.py:283
  153.7 0.2 copy.8
  153.8 0.9 copy.9
  (1 shorter events, 0.0 us)
Async XLA Ops:
  3.0 81.6 %copy-start = (s32[1,64,64]{2,1,0:T(8,128)S(1)}, s32[1,64,64]{2,1,0:T(8,128)}, u32[]{:S(2)}) copy-start(s32[1,64,64]{2,1,0:T(8,128)} %param.11) | copy-start | bytes 49156
  3.0 81.6 %copy-start.1 = (s32[8]{0:T(128)S(1)}, s32[8]{0:T(128)}, u32[]{:S(2)}) copy-start(s32[8]{0:T(128)} %lengths_ref.3) | copy-start | bytes 100
  84.6 40.3 %copy-start.2 = (f32[1024]{0:T(1024)S(1)}, f32[1024]{0:T(1024)}, u32[]{:S(2)}) copy-start(f32[1024]{0:T(1024)} %param.13) | copy-start | bytes 12292
  118.2 23.6 %all-to-all-start.2 = ((f32[64,1,512]{2,1,0:T(1,128)}), f32[64,1,512]{2,1,0:T(1,128)S(1)}, u32[]{:S(2)}, u32[]{:S(2)}) async-start(f32[64,1,512]{2,1,0:T(1,128)} %shard_map.75), calls=%async_computation.2 | async-start | bytes 262144 | tf_op jit(solution)/shard_map/all_to_all | solution.py:279

commit v4 on v3

--- a/solution.py
+++ b/solution.py
@@ -18,7 +18,7 @@
 EPSILON = 1e-05
 CTX = ("y", "zh", "zl")
 REGROUP = ("zl", "zh", "y")
-CHUNKS = ("node", "y", "zh")
+CHUNKS = ("zh", "node", "y")
 PRECISE = lax.Precision.HIGHEST
 F32 = jnp.float32
 BF16 = jnp.bfloat16
@@ -112,8 +112,12 @@
     return jnp.sum(jnp.where(inside, target, 0.0), axis=0, keepdims=True).astype(jnp.int32) - 1
 
 
-def unpack(targets, received):
-    pick = (iota((CHUNK, OWNERS * CAP), 0) == targets).astype(F32).astype(BF16)
+def place_kernel(matrix_ref, pick_ref):
+    targets = slot_targets(matrix_ref)
+    pick_ref[...] = (iota((CHUNK, OWNERS * CAP), 0) == targets).astype(F32).astype(BF16)
+
+
+def unpack(pick, received):
     return dot(pick, received.reshape(OWNERS * CAP, received.shape[2])).astype(BF16)
 
 
@@ -134,10 +138,8 @@
     return doc_of(lengths_ref, jnp.full((1, 1), place, jnp.int32))
 
 
-def maps_kernel(lengths_ref, matrix_ref, received_ref, rows_ref, targets_ref, map_ref):
-    targets = slot_targets(matrix_ref)
-    targets_ref[...] = targets
-    rows_ref[...] = unpack(targets, received_ref[:, :, :LATE])
+def maps_kernel(lengths_ref, pick_ref, received_ref, rows_ref, map_ref):
+    rows_ref[...] = unpack(pick_ref[...], received_ref[:, :, :LATE])
     first = chunk_start()
     parts = decays(rows_ref[:, DK : 2 * DK])
     after = jnp.zeros((1, DK), F32)
@@ -158,9 +160,9 @@
     map_ref[:, 0, 2 * DV :] = jnp.where(iota((half, DK), 1) < half, kept[:half], kept[half:])
 
 
-def block_kernel(lengths_ref, targets_ref, received_ref, rows_ref, partial_ref, query_out_ref):
+def block_kernel(lengths_ref, pick_ref, received_ref, rows_ref, partial_ref, query_out_ref):
     first = chunk_start()
-    queries = unpack(targets_ref[...], received_ref[:, :, LATE:])
+    queries = unpack(pick_ref[...], received_ref[:, :, LATE:])
     state = None
     passed = jnp.zeros((1, DK), F32)
     chunk_before = doc_at(lengths_ref, first - 1)
@@ -202,17 +204,29 @@
 
 
 def scan_kernel(map_ref, prefix_ref):
-    low = iota((1, DK), 1) < DK // 2
-
-    def step(chunk, state):
-        prefix_ref[chunk] = state
-        here = map_ref[chunk]
-        kept = here[:, 2 * DV :]
-        other = pltpu.roll(kept, DK // 2, 1)
-        one, two = jnp.where(low, kept, other), jnp.where(low, other, kept)
-        return jnp.concatenate([one, one, two, two], axis=1) * state + here[:, : 2 * DV]
-
-    lax.fori_loop(0, map_ref.shape[0], step, jnp.zeros((1, 2 * DV), F32), unroll=True)
+    rows = map_ref.shape[0] // GROUP
+    low = iota((rows, DK), 1) < DK // 2
+    state = jnp.zeros((rows, 2 * DV), F32)
+    kept = jnp.ones((rows, 2 * DV), F32)
+    inside = []
+    for nth in range(GROUP):
+        inside.append((kept, state))
+        here = map_ref[nth * rows : (nth + 1) * rows, 0, :]
+        own = here[:, 2 * DV :]
+        other = pltpu.roll(own, DK // 2, 1)
+        one, two = jnp.where(low, own, other), jnp.where(low, other, own)
+        own = jnp.concatenate([one, one, two, two], axis=1)
+        state = own * state + here[:, : 2 * DV]
+        kept = own * kept
+    row = iota((rows, 2 * DV), 0)
+    step = 1
+    while step < rows:
+        state = kept * jnp.where(row < step, 0.0, pltpu.roll(state, step, 0)) + state
+        kept = kept * jnp.where(row < step, 1.0, pltpu.roll(kept, step, 0))
+        step *= 2
+    before = jnp.where(row < 1, 0.0, pltpu.roll(state, 1, 0))
+    for nth, (kept, state) in enumerate(inside):
+        prefix_ref[nth * rows : (nth + 1) * rows, 0, :] = kept * before + state
 
 
 def finish_kernel(prefix_ref, partial_ref, query_ref, gain_ref, out_ref):
@@ -258,23 +272,20 @@
         65500000,
     )(*streams)
     received = lax.all_to_all(packed.reshape(OWNERS, CAP, WIDTH), REGROUP, 0, 0, tiled=True)
-    rows, targets, maps = call(
+    pick = call(place_kernel, [VMEM], shape((CHUNK, OWNERS * CAP), BF16), 1 << 28)(matrix)
+    rows, maps = call(
         maps_kernel,
         [SMEM, VMEM, VMEM],
-        (
-            shape((CHUNK, LATE), BF16),
-            shape((1, OWNERS * CAP), jnp.int32),
-            shape((OWNERS, 1, 2 * DV + DK)),
-        ),
+        (shape((CHUNK, LATE), BF16), shape((OWNERS, 1, 2 * DV + DK))),
         1 << 29,
-    )(doc_lengths, matrix, received)
+    )(doc_lengths, pick, received)
     maps = lax.all_to_all(maps, CHUNKS, 0, 0, tiled=True)
     partial, query = call(
         block_kernel,
         [SMEM, VMEM, VMEM, VMEM],
         (shape((CHUNK, DV)), shape((CHUNK, DK))),
         1 << 30,
-    )(doc_lengths, targets, received, rows)
+    )(doc_lengths, pick, received, rows)
     prefix = call(scan_kernel, [VMEM], shape((OWNERS, 1, 2 * DV)), 1 << 24)(maps)
     prefix = lax.all_to_all(prefix, CHUNKS, 0, 0, tiled=True)
     out = call(finish_kernel, [VMEM] * 4, shape((GROUP, TOK, DV), BF16), 1 << 28)(

time: 156 us -> 155 us (level)
  blocking collectives: 123 us -> 40.5 us
  waiting for transfers between devices: 13.6 us -> 73.2 us
  starting transfers between devices: 6.69 us -> 26.7 us
    all_to_all x1 -> x0, blocking collectives: 81.6 us -> none  [local(): lax.all_to_all(packed.reshape(OWNERS, CAP, WIDTH), REGROUP, 0, 0, tiled=T...]
    all_to_all x0 -> x1, waiting for transfers between devices: none -> 62 us  [local(): lax.all_to_all(packed.reshape(OWNERS, CAP, WIDTH), REGROUP, 0, 0, tiled=T...]
    all_to_all x0 -> x1, starting transfers between devices: none -> 18.7 us  [local(): lax.all_to_all(packed.reshape(OWNERS, CAP, WIDTH), REGROUP, 0, 0, tiled=T...]
    all_to_all x1, waiting for transfers between devices: 13.6 us -> 11.2 us  [local(): prefix = lax.all_to_all(prefix, CHUNKS, 0, 0, tiled=True)]
  transfers between devices with their start and end apart: 1 -> 2, of which waited for: 1 -> 2; matrix products, arithmetic and copies ran while one was open for 0% -> 0% of each run, Pallas kernels for 2% -> 3%
where the time goes in v4:
time: 155 us; the launch traced here: 153 us
  waiting for transfers between devices  73.2 us (47%)
  blocking collectives  40.5 us (26%)
  starting transfers between devices  26.7 us (17%)
  Pallas kernels  10.7 us (7%)
  local copies, waits for them, and re-layouts  2.09 us (1%)
    all_to_all x1, waiting for transfers between devices, local(): lax.all_to_all(packed.reshape(OWNERS, CAP, WIDTH), REGROUP, 0, 0, tiled=T...  62 us
    all_to_all x1, blocking collectives, local(): maps = lax.all_to_all(maps, CHUNKS, 0, 0, tiled=True)  29.4 us
    all_to_all x1, starting transfers between devices, local(): lax.all_to_all(packed.reshape(OWNERS, CAP, WIDTH), REGROUP, 0, 0, tiled=T...  18.7 us
    all_to_all x1, waiting for transfers between devices, local(): prefix = lax.all_to_all(prefix, CHUNKS, 0, 0, tiled=True)  11.2 us
    all_to_all x1, blocking collectives, local(): out = lax.all_to_all(out, 'zl', 0, 0, tiled=True)  11.1 us
    all_to_all x1, starting transfers between devices, local(): prefix = lax.all_to_all(prefix, CHUNKS, 0, 0, tiled=True)  7.99 us
    pallas_call x1, Pallas kernels, local(): call(block_kernel, [SMEM, VMEM, VMEM, VMEM], (shape((CHUNK, DV)), shape((...  3.25 us
  transfers between devices with their start and end apart: 2, of which 2 were waited for; matrix products, arithmetic and copies ran while one was open for 0% of the time, Pallas kernels for 3%

profile of v4, /device:TPU:6, one launch (start us, length us, event | category | flops | bytes accessed | tf_op | source)
XLA Modules:
  0.0 153.3 jit_solution(8333175101124614449)
XLA Ops:
  0.0 3.0 %shard_map.74 = bf16[4,16,16,640]{3,2,1,0:T(8,128)(2,1)} custom-call(s32[64,64]{1,0:T(8,128)} %bitcast.8, bf16[128,512]{1,0:T(8,128)(2,1)} %bitcast.14, bf16[128,512]{1,0:T(8,128)(2,1)} %bitcast.15, bf16[128,1024]{1,0:T(8,128)(2,1)} %bitcast.13, bf16[128,512]{1,0:T(8,128)(2,1)} %bitcast.16), custom_call_target="tpu_custom_call" | custom-call | flops 268435456 | bytes 1048576 | tf_op jit(solution)/shard_map/pallas_call | solution.py:266
  3.0 0.0 copy-start
  3.0 0.0 copy-start.1
  3.0 18.7 %all-to-all-start = ((bf16[64,16,640]{2,1,0:T(8,128)(2,1)}), bf16[64,16,640]{2,1,0:T(8,128)(2,1)S(1)}, u32[]{:S(2)}, u32[]{:S(2)}) async-start(bf16[64,16,640]{2,1,0:T(8,128)(2,1)} %bitcast.10), calls=%async_computation | async-start | bytes 2621440 | tf_op jit(solution)/shard_map/all_to_all | solution.py:274
  21.8 0.0 copy-done
  21.8 0.9 shard_map.73.pick_ref
  22.6 0.0 copy-start.4
  22.6 62.0 %all-to-all-done.received_ref = bf16[64,16,640]{2,1,0:T(8,128)(2,1)S(1)} async-done(((bf16[64,16,640]{2,1,0:T(8,128)(2,1)}), bf16[64,16,640]{2,1,0:T(8,128)(2,1)S(1)}, u32[]{:S(2)}, u32[]{:S(2)}) %all-to-all-start) | async-done | bytes 1310752 | tf_op jit(solution)/shard_map/all_to_all | solution.py:274
  84.6 0.0 copy-done.1
  84.6 2.1 %shard_map.75 = (bf16[512,512]{1,0:T(8,128)(2,1)S(1)}, f32[64,1,640]{2,1,0:T(1,128)S(1)}) custom-call(s32[8]{0:T(128)S(1)} %copy-done.1, bf16[512,1024]{1,0:T(8,128)(2,1)S(1)} %shard_map.73.pick_ref, bf16[64,16,640]{2,1,0:T(8,128)(2,1)S(1)} %all-to-all-done.received_ref), custom_call_target="tpu_custom_call" | custom-call | flops 536870912 | bytes 1048576 | tf_op jit(solution)/shard_map/pallas_call | solution.py:276
  86.8 0.0 copy-start.2
  86.8 29.4 %all_to_all.20.map_ref = f32[64,1,640]{2,1,0:T(1,128)S(1)} all-to-all(f32[64,1,640]{2,1,0:T(1,128)S(1)} %get-tuple-element.9), channel_id=1, replica_groups=mesh['y'=4,'zh'=4,'zl'=4,'node'=4,'tp'=2] {'zh','node','y'}, dimensions={0} | all-to-all | bytes 327680 | tf_op jit(solution)/shard_map/all_to_all | solution.py:282
  116.2 0.8 shard_map.76
  117.0 0.0 copy-done.2
  117.0 8.0 %all-to-all-start.2 = ((f32[64,1,512]{2,1,0:T(1,128)}), f32[64,1,512]{2,1,0:T(1,128)S(1)}, u32[]{:S(2)}, u32[]{:S(2)}) async-start(f32[64,1,512]{2,1,0:T(1,128)} %shard_map.76), calls=%async_computation.2 | async-start | bytes 262144 | tf_op jit(solution)/shard_map/all_to_all | solution.py:290
  125.0 0.0 copy-done.4
  125.0 0.0 copy-start.3
  125.0 1.0 copy-done.3
  126.1 3.2 %shard_map.77 = (f32[512,256]{1,0:T(8,128)S(1)}, f32[512,128]{1,0:T(8,128)S(1)}) custom-call(s32[8]{0:T(128)S(1)} %copy-done.1, bf16[512,1024]{1,0:T(8,128)(2,1)S(1)} %shard_map.73.pick_ref, bf16[64,16,640]{2,1,0:T(8,128)(2,1)S(1)} %all-to-all-done.received_ref, bf16[512,512]{1,0:T(8,128)(2,1)S(1)} %copy-done.3), custom_call_target="tpu_custom_call" | custom-call | flops 1073741824 | bytes 1048576 | tf_op jit(solution)/shard_map/pallas_call | solution.py:283
  129.3 11.2 %all-to-all-done.2.prefix_ref = f32[64,1,512]{2,1,0:T(1,128)S(1)} async-done(((f32[64,1,512]{2,1,0:T(1,128)}), f32[64,1,512]{2,1,0:T(1,128)S(1)}, u32[]{:S(2)}, u32[]{:S(2)}) %all-to-all-start.2) | async-done | bytes 131104 | tf_op jit(solution)/shard_map/all_to_all | solution.py:290
  140.5 0.7 shard_map.78
  141.2 11.1 %all_to_all.21 = bf16[4,128,256]{2,1,0:T(8,128)(2,1)S(1)} all-to-all(bf16[4,128,256]{2,1,0:T(8,128)(2,1)S(1)} %shard_map.78), channel_id=1, replica_groups=mesh['y'=4,'zh'=4,'zl'=4,'node'=4,'tp'=2] {'zl'}, dimensions={0} | all-to-all | bytes 524288 | tf_op jit(solution)/shard_map/all_to_all | solution.py:294
  152.3 0.2 copy.8
  152.4 0.9 copy.9
  (1 shorter events, 0.0 us)
Async XLA Ops:
  3.0 18.8 %copy-start = (s32[1,64,64]{2,1,0:T(8,128)S(1)}, s32[1,64,64]{2,1,0:T(8,128)}, u32[]{:S(2)}) copy-start(s32[1,64,64]{2,1,0:T(8,128)} %param.11) | copy-start | bytes 49156
  3.0 81.6 %copy-start.1 = (s32[8]{0:T(128)S(1)}, s32[8]{0:T(128)}, u32[]{:S(2)}) copy-start(s32[8]{0:T(128)} %lengths_ref.3) | copy-start | bytes 100
  3.0 81.6 %all-to-all-start = ((bf16[64,16,640]{2,1,0:T(8,128)(2,1)}), bf16[64,16,640]{2,1,0:T(8,128)(2,1)S(1)}, u32[]{:S(2)}, u32[]{:S(2)}) async-start(bf16[64,16,640]{2,1,0:T(8,128)(2,1)} %bitcast.10), calls=%async_computation | async-start | bytes 2621440 | tf_op jit(solution)/shard_map/all_to_all | solution.py:274
  22.6 102.4 %copy-start.4 = (f32[1024]{0:T(1024)S(1)}, f32[1024]{0:T(1024)}, u32[]{:S(2)}) copy-start(f32[1024]{0:T(1024)} %param.13) | copy-start | bytes 12292
  86.8 30.3 %copy-start.2 = (bf16[512,512]{1,0:T(8,128)(2,1)}, bf16[512,512]{1,0:T(8,128)(2,1)S(1)}, u32[]{:S(2)}) copy-start(bf16[512,512]{1,0:T(8,128)(2,1)S(1)} %get-tuple-element.10.rows_ref) | copy-start | bytes 1572868
  117.0 23.5 %all-to-all-start.2 = ((f32[64,1,512]{2,1,0:T(1,128)}), f32[64,1,512]{2,1,0:T(1,128)S(1)}, u32[]{:S(2)}, u32[]{:S(2)}) async-start(f32[64,1,512]{2,1,0:T(1,128)} %shard_map.76), calls=%async_computation.2 | async-start | bytes 262144 | tf_op jit(solution)/shard_map/all_to_all | solution.py:290
  125.0 1.0 copy-start.3

commit v5 on v4

--- a/solution.py
+++ b/solution.py
@@ -18,7 +18,7 @@
 EPSILON = 1e-05
 CTX = ("y", "zh", "zl")
 REGROUP = ("zl", "zh", "y")
-CHUNKS = ("zh", "node", "y")
+CHUNKS = ("zl", "node", "y")
 PRECISE = lax.Precision.HIGHEST
 F32 = jnp.float32
 BF16 = jnp.bfloat16
@@ -68,12 +68,12 @@
         rows = dot(pick, ref[...]).astype(BF16)
         for head in range(HEADS):
             piece = rows[:, head * width : (head + 1) * width]
-            out_ref[head, :, :, at : at + width] = piece.reshape(slots // CAP, CAP, width)
+            out_ref[:, head, :, :, at : at + width] = piece.reshape(4, 4, CAP, width)
         at += width
 
 
 def chunk_in_group():
-    return lax.axis_index("y") * 4 + lax.axis_index("zh")
+    return lax.axis_index("y") * 4 + lax.axis_index("zl")
 
 
 def chunk_start():
@@ -112,9 +112,13 @@
     return jnp.sum(jnp.where(inside, target, 0.0), axis=0, keepdims=True).astype(jnp.int32) - 1
 
 
-def place_kernel(matrix_ref, pick_ref):
-    targets = slot_targets(matrix_ref)
-    pick_ref[...] = (iota((CHUNK, OWNERS * CAP), 0) == targets).astype(F32).astype(BF16)
+def picked(targets):
+    return (iota((CHUNK, OWNERS * CAP), 0) == targets).astype(F32).astype(BF16)
+
+
+def place_kernel(matrix_ref, targets_ref, pick_ref):
+    targets_ref[...] = slot_targets(matrix_ref)
+    pick_ref[...] = picked(targets_ref[...])
 
 
 def unpack(pick, received):
@@ -160,9 +164,9 @@
     map_ref[:, 0, 2 * DV :] = jnp.where(iota((half, DK), 1) < half, kept[:half], kept[half:])
 
 
-def block_kernel(lengths_ref, pick_ref, received_ref, rows_ref, partial_ref, query_out_ref):
+def block_kernel(lengths_ref, targets_ref, received_ref, rows_ref, partial_ref, query_out_ref):
     first = chunk_start()
-    queries = unpack(pick_ref[...], received_ref[:, :, LATE:])
+    queries = unpack(picked(targets_ref[...]), received_ref[:, :, LATE:])
     state = None
     passed = jnp.zeros((1, DK), F32)
     chunk_before = doc_at(lengths_ref, first - 1)
@@ -229,14 +233,21 @@
         prefix_ref[nth * rows : (nth + 1) * rows, 0, :] = kept * before + state
 
 
-def finish_kernel(prefix_ref, partial_ref, query_ref, gain_ref, out_ref):
+def finish_kernel(prefix_ref, partial_ref, query_ref, gain_ref, *out_refs):
     state = jnp.concatenate([prefix_ref[:, 0, :DV], prefix_ref[:, 0, DV:]], axis=0)
-    gain = gain_ref[pl.ds(lax.axis_index("zl"), 1), :]
-    for block in range(GROUP):
-        span = slice(block * TOK, (block + 1) * TOK)
+    head = lax.axis_index("zh")
+    gain = gain_ref[pl.ds(head, 1), :]
+    for turn, out_ref in enumerate(out_refs):
+        span = pl.ds(pl.multiple_of(((head + turn) & 3) * TOK, TOK), TOK)
         mixed = partial_ref[span, :] + dot(query_ref[span, :], state, precision=PRECISE)
         scale = lax.rsqrt(jnp.mean(mixed * mixed, axis=1, keepdims=True) + EPSILON)
-        out_ref[block] = (mixed * scale * gain).astype(BF16)
+        out_ref[...] = (mixed * scale * gain).astype(BF16)
+
+
+def join_kernel(*refs):
+    for turn, ref in enumerate(refs[:-1]):
+        head = (lax.axis_index("zl") - turn) & 3
+        refs[-1][:, pl.ds(pl.multiple_of(head * DV, DV), DV)] = ref[...]
 
 
 SMEM = pl.BlockSpec(memory_space=pltpu.SMEM)
@@ -266,13 +277,18 @@
     packed = call(
         pack_kernel,
         [HBM] * 5,
-        shape((HEADS, OWNERS // GROUP, CAP, WIDTH), BF16),
+        shape((4, HEADS, 4, CAP, WIDTH), BF16),
         1 << 28,
         [pltpu.VMEM(a.shape, a.dtype) for a in streams] + [pltpu.SemaphoreType.DMA((5,))],
         65500000,
     )(*streams)
     received = lax.all_to_all(packed.reshape(OWNERS, CAP, WIDTH), REGROUP, 0, 0, tiled=True)
-    pick = call(place_kernel, [VMEM], shape((CHUNK, OWNERS * CAP), BF16), 1 << 28)(matrix)
+    targets, pick = call(
+        place_kernel,
+        [VMEM],
+        (shape((1, OWNERS * CAP), jnp.int32), shape((CHUNK, OWNERS * CAP), BF16)),
+        1 << 28,
+    )(matrix)
     rows, maps = call(
         maps_kernel,
         [SMEM, VMEM, VMEM],
@@ -285,14 +301,21 @@
         [SMEM, VMEM, VMEM, VMEM],
         (shape((CHUNK, DV)), shape((CHUNK, DK))),
         1 << 30,
-    )(doc_lengths, pick, received, rows)
+    )(doc_lengths, targets, received, rows)
     prefix = call(scan_kernel, [VMEM], shape((OWNERS, 1, 2 * DV)), 1 << 24)(maps)
     prefix = lax.all_to_all(prefix, CHUNKS, 0, 0, tiled=True)
-    out = call(finish_kernel, [VMEM] * 4, shape((GROUP, TOK, DV), BF16), 1 << 28)(
+    parts = call(finish_kernel, [VMEM] * 4, [shape((TOK, DV), BF16)] * GROUP, 1 << 28)(
         prefix, partial, query, norm_gain.reshape(HEADS, DV)
     )
-    out = lax.all_to_all(out, "zl", 0, 0, tiled=True)
-    return jnp.transpose(out, (1, 0, 2)).reshape(1, TOK, HEADS * DV)
+    pairs = [(head, nth) for head in range(HEADS) for nth in range(GROUP)]
+    parts = [
+        lax.ppermute(
+            part, ("zh", "zl"), [(h * 4 + nth, nth * 4 + (h + turn) % 4) for h, nth in pairs]
+        )
+        for turn, part in enumerate(parts)
+    ]
+    out = call(join_kernel, [VMEM] * GROUP, shape((TOK, HEADS * DV), BF16))(*parts)
+    return out.reshape(1, TOK, HEADS * DV)
 
 
 def solution(mesh):

time: 155 us -> 151 us (0.974)
  the two profiles are of different devices: /device:TPU:6 before, /device:TPU:32 now
where the time goes in v5:
time: 151 us
  waiting for transfers between devices  75.8 us (50%)
  starting transfers between devices  46.6 us (31%)
  blocking collectives  16.7 us (11%)
  Pallas kernels  11.4 us (8%)
    all_to_all x1, waiting for transfers between devices, local(): lax.all_to_all(packed.reshape(OWNERS, CAP, WIDTH), REGROUP, 0, 0, tiled=T...  66 us
    ppermute x4, starting transfers between devices, local(): lax.ppermute(part, ('zh', 'zl'), [(h * 4 + nth, nth * 4 + (h + turn) % 4)...  22.3 us
    all_to_all x1, starting transfers between devices, local(): lax.all_to_all(packed.reshape(OWNERS, CAP, WIDTH), REGROUP, 0, 0, tiled=T...  18.4 us
    all_to_all x1, blocking collectives, local(): maps = lax.all_to_all(maps, CHUNKS, 0, 0, tiled=True)  16.7 us
    all_to_all x1, waiting for transfers between devices, local(): prefix = lax.all_to_all(prefix, CHUNKS, 0, 0, tiled=True)  6.24 us
    all_to_all x1, starting transfers between devices, local(): prefix = lax.all_to_all(prefix, CHUNKS, 0, 0, tiled=True)  5.94 us
    ppermute x4, waiting for transfers between devices, local(): lax.ppermute(part, ('zh', 'zl'), [(h * 4 + nth, nth * 4 + (h + turn) % 4)...  3.54 us
    pallas_call x1, Pallas kernels, local(): call(block_kernel, [SMEM, VMEM, VMEM, VMEM], (shape((CHUNK, DV)), shape((...  3.25 us
  transfers between devices with their start and end apart: 6, of which 3 were waited for; matrix products, arithmetic and copies ran while one was open for 0% of the time, Pallas kernels for 3%

profile of v5, /device:TPU:32, one launch (start us, length us, event | category | flops | bytes accessed | tf_op | source)
XLA Modules:
  0.0 150.7 jit_solution(10270826606136151929)
XLA Ops:
  0.0 3.0 %shard_map.74 = bf16[4,4,4,16,640]{4,3,2,1,0:T(8,128)(2,1)} custom-call(s32[64,64]{1,0:T(8,128)} %bitcast.7, bf16[128,512]{1,0:T(8,128)(2,1)} %bitcast.11, bf16[128,512]{1,0:T(8,128)(2,1)} %bitcast.12, bf16[128,1024]{1,0:T(8,128)(2,1)} %bitcast.10, bf16[128,512]{1,0:T(8,128)(2,1)} %bitcast.13), custom_call_target="tpu_custom_call" | custom-call | flops 268435456 | bytes 1048576 | tf_op jit(solution)/shard_map/pallas_call | solution.py:277
  3.0 0.0 copy-start
  3.0 0.0 copy-start.1
  3.0 18.4 %all-to-all-start = ((bf16[64,16,640]{2,1,0:T(8,128)(2,1)}), bf16[64,16,640]{2,1,0:T(8,128)(2,1)S(1)}, u32[]{:S(2)}, u32[]{:S(2)}) async-start(bf16[64,16,640]{2,1,0:T(8,128)(2,1)} %bitcast.9), calls=%async_computation | async-start | bytes 2621440 | tf_op jit(solution)/shard_map/all_to_all | solution.py:285
  21.4 0.0 copy-done
  21.4 0.8 shard_map.73
  22.3 66.0 %all-to-all-done.received_ref = bf16[64,16,640]{2,1,0:T(8,128)(2,1)S(1)} async-done(((bf16[64,16,640]{2,1,0:T(8,128)(2,1)}), bf16[64,16,640]{2,1,0:T(8,128)(2,1)S(1)}, u32[]{:S(2)}, u32[]{:S(2)}) %all-to-all-start) | async-done | bytes 1310752 | tf_op jit(solution)/shard_map/all_to_all | solution.py:285
  88.3 0.0 copy-done.1
  88.3 0.0 copy-start.2
  88.3 2.1 %shard_map.75 = (bf16[512,512]{1,0:T(8,128)(2,1)S(1)}, f32[64,1,640]{2,1,0:T(1,128)S(1)}) custom-call(s32[8]{0:T(128)S(1)} %copy-done.1, bf16[512,1024]{1,0:T(8,128)(2,1)S(1)} %get-tuple-element.15.pick_ref, bf16[64,16,640]{2,1,0:T(8,128)(2,1)S(1)} %all-to-all-done.received_ref), custom_call_target="tpu_custom_call" | custom-call | flops 536870912 | bytes 1048576 | tf_op jit(solution)/shard_map/pallas_call | solution.py:292
  90.4 16.7 %all_to_all.15.map_ref = f32[64,1,640]{2,1,0:T(1,128)S(1)} all-to-all(f32[64,1,640]{2,1,0:T(1,128)S(1)} %get-tuple-element.16), channel_id=1, replica_groups=mesh['y'=4,'zh'=4,'zl'=4,'node'=4,'tp'=2] {'zl','node','y'}, dimensions={0} | all-to-all | bytes 327680 | tf_op jit(solution)/shard_map/all_to_all | solution.py:298
  107.1 0.8 shard_map.76
  107.9 5.9 %all-to-all-start.2 = ((f32[64,1,512]{2,1,0:T(1,128)}), f32[64,1,512]{2,1,0:T(1,128)S(1)}, u32[]{:S(2)}, u32[]{:S(2)}) async-start(f32[64,1,512]{2,1,0:T(1,128)} %shard_map.76), calls=%async_computation.2 | async-start | bytes 262144 | tf_op jit(solution)/shard_map/all_to_all | solution.py:306
  113.8 0.0 copy-done.2
  113.9 3.3 %shard_map.77 = (f32[512,256]{1,0:T(8,128)S(1)}, f32[512,128]{1,0:T(8,128)S(1)}) custom-call(s32[8]{0:T(128)S(1)} %copy-done.1, s32[1,1024]{1,0:T(1,128)S(1)} %get-tuple-element.17.targets_ref, bf16[64,16,640]{2,1,0:T(8,128)(2,1)S(1)} %all-to-all-done.received_ref, bf16[512,512]{1,0:T(8,128)(2,1)S(1)} %get-tuple-element.18.rows_ref), custom_call_target="tpu_custom_call" | custom-call | flops 1073741824 | bytes 1048576 | tf_op jit(solution)/shard_map/pallas_call | solution.py:299
  117.1 6.2 %all-to-all-done.2.prefix_ref = f32[64,1,512]{2,1,0:T(1,128)S(1)} async-done(((f32[64,1,512]{2,1,0:T(1,128)}), f32[64,1,512]{2,1,0:T(1,128)S(1)}, u32[]{:S(2)}, u32[]{:S(2)}) %all-to-all-start.2) | async-done | bytes 131104 | tf_op jit(solution)/shard_map/all_to_all | solution.py:306
  123.4 0.7 shard_map.78
  124.1 3.0 %collective-permute-start = (bf16[128,256]{1,0:T(8,128)(2,1)S(1)}, bf16[128,256]{1,0:T(8,128)(2,1)S(1)}, u32[]{:S(2)}, u32[]{:S(2)}) collective-permute-start(bf16[128,256]{1,0:T(8,128)(2,1)S(1)} %get-tuple-element.21), channel_id=1, source_target_pairs={{0,0},{8,32},{16,64},{24,96},{32,8},{40,40},{48,72},{56,104},{64,1... | collective-permute-start | bytes 196616 | tf_op jit(solution)/shard_map/ppermute | solution.py:312
  127.1 1.9 %collective-permute-start.1 = (bf16[128,256]{1,0:T(8,128)(2,1)S(1)}, bf16[128,256]{1,0:T(8,128)(2,1)S(1)}, u32[]{:S(2)}, u32[]{:S(2)}) collective-permute-start(bf16[128,256]{1,0:T(8,128)(2,1)S(1)} %get-tuple-element.22), channel_id=1, source_target_pairs={{0,8},{8,40},{16,72},{24,104},{32,16},{40,48},{48,80},{56,112},{64... | collective-permute-start | bytes 196616 | tf_op jit(solution)/shard_map/ppermute | solution.py:312
  129.0 5.4 %collective-permute-start.2 = (bf16[128,256]{1,0:T(8,128)(2,1)S(1)}, bf16[128,256]{1,0:T(8,128)(2,1)S(1)}, u32[]{:S(2)}, u32[]{:S(2)}) collective-permute-start(bf16[128,256]{1,0:T(8,128)(2,1)S(1)} %get-tuple-element.23), channel_id=1, source_target_pairs={{0,16},{8,48},{16,80},{24,112},{32,24},{40,56},{48,88},{56,120},{6... | collective-permute-start | bytes 196616 | tf_op jit(solution)/shard_map/ppermute | solution.py:312
  134.4 12.0 %collective-permute-start.3 = (bf16[128,256]{1,0:T(8,128)(2,1)S(1)}, bf16[128,256]{1,0:T(8,128)(2,1)S(1)}, u32[]{:S(2)}, u32[]{:S(2)}) collective-permute-start(bf16[128,256]{1,0:T(8,128)(2,1)S(1)} %get-tuple-element.24), channel_id=1, source_target_pairs={{0,24},{8,56},{16,88},{24,120},{32,0},{40,32},{48,64},{56,96},{64,... | collective-permute-start | bytes 196616 | tf_op jit(solution)/shard_map/ppermute | solution.py:312
  146.4 0.0 collective-permute-done.refs_0_
  146.4 0.0 collective-permute-done.1.refs_1_
  146.4 0.0 collective-permute-done.2.refs_2_
  146.4 3.5 %collective-permute-done.3.refs_3_ = bf16[128,256]{1,0:T(8,128)(2,1)S(1)} collective-permute-done((bf16[128,256]{1,0:T(8,128)(2,1)S(1)}, bf16[128,256]{1,0:T(8,128)(2,1)S(1)}, u32[]{:S(2)}, u32[]{:S(2)}) %collective-permute-start.3) | collective-permute-done | bytes 65568 | tf_op jit(solution)/shard_map/ppermute | solution.py:312
  149.9 0.7 shard_map.79
  (1 shorter events, 0.0 us)
Async XLA Ops:
  3.0 18.4 %copy-start = (s32[1,64,64]{2,1,0:T(8,128)S(1)}, s32[1,64,64]{2,1,0:T(8,128)}, u32[]{:S(2)}) copy-start(s32[1,64,64]{2,1,0:T(8,128)} %param.11) | copy-start | bytes 49156
  3.0 85.3 %copy-start.1 = (s32[8]{0:T(128)S(1)}, s32[8]{0:T(128)}, u32[]{:S(2)}) copy-start(s32[8]{0:T(128)} %lengths_ref.3) | copy-start | bytes 100
  3.0 85.3 %all-to-all-start = ((bf16[64,16,640]{2,1,0:T(8,128)(2,1)}), bf16[64,16,640]{2,1,0:T(8,128)(2,1)S(1)}, u32[]{:S(2)}, u32[]{:S(2)}) async-start(bf16[64,16,640]{2,1,0:T(8,128)(2,1)} %bitcast.9), calls=%async_computation | async-start | bytes 2621440 | tf_op jit(solution)/shard_map/all_to_all | solution.py:285
  88.3 25.5 %copy-start.2 = (f32[1024]{0:T(1024)S(1)}, f32[1024]{0:T(1024)}, u32[]{:S(2)}) copy-start(f32[1024]{0:T(1024)} %param.13) | copy-start | bytes 12292
  107.9 15.5 %all-to-all-start.2 = ((f32[64,1,512]{2,1,0:T(1,128)}), f32[64,1,512]{2,1,0:T(1,128)S(1)}, u32[]{:S(2)}, u32[]{:S(2)}) async-start(f32[64,1,512]{2,1,0:T(1,128)} %shard_map.76), calls=%async_computation.2 | async-start | bytes 262144 | tf_op jit(solution)/shard_map/all_to_all | solution.py:306
  124.1 22.3 %collective-permute-start = (bf16[128,256]{1,0:T(8,128)(2,1)S(1)}, bf16[128,256]{1,0:T(8,128)(2,1)S(1)}, u32[]{:S(2)}, u32[]{:S(2)}) collective-permute-start(bf16[128,256]{1,0:T(8,128)(2,1)S(1)} %get-tuple-element.21), channel_id=1, source_target_pairs={{0,0},{8,32},{16,64},{24,96},{32,8},{40,40},{48,72},{56,104},{64,1... | collective-permute-start | bytes 196616 | tf_op jit(solution)/shard_map/ppermute | solution.py:312
  127.1 19.3 %collective-permute-start.1 = (bf16[128,256]{1,0:T(8,128)(2,1)S(1)}, bf16[128,256]{1,0:T(8,128)(2,1)S(1)}, u32[]{:S(2)}, u32[]{:S(2)}) collective-permute-start(bf16[128,256]{1,0:T(8,128)(2,1)S(1)} %get-tuple-element.22), channel_id=1, source_target_pairs={{0,8},{8,40},{16,72},{24,104},{32,16},{40,48},{48,80},{56,112},{64... | collective-permute-start | bytes 196616 | tf_op jit(solution)/shard_map/ppermute | solution.py:312
  129.0 17.4 %collective-permute-start.2 = (bf16[128,256]{1,0:T(8,128)(2,1)S(1)}, bf16[128,256]{1,0:T(8,128)(2,1)S(1)}, u32[]{:S(2)}, u32[]{:S(2)}) collective-permute-start(bf16[128,256]{1,0:T(8,128)(2,1)S(1)} %get-tuple-element.23), channel_id=1, source_target_pairs={{0,16},{8,48},{16,80},{24,112},{32,24},{40,56},{48,88},{56,120},{6... | collective-permute-start | bytes 196616 | tf_op jit(solution)/shard_map/ppermute | solution.py:312
  134.4 15.6 %collective-permute-start.3 = (bf16[128,256]{1,0:T(8,128)(2,1)S(1)}, bf16[128,256]{1,0:T(8,128)(2,1)S(1)}, u32[]{:S(2)}, u32[]{:S(2)}) collective-permute-start(bf16[128,256]{1,0:T(8,128)(2,1)S(1)} %get-tuple-element.24), channel_id=1, source_target_pairs={{0,24},{8,56},{16,88},{24,120},{32,0},{40,32},{48,64},{56,96},{64,... | collective-permute-start | bytes 196616 | tf_op jit(solution)/shard_map/ppermute | solution.py:312

commit v6 on v5

--- a/solution.py
+++ b/solution.py
@@ -17,7 +17,7 @@
 WIDTH = LATE + DK
 EPSILON = 1e-05
 CTX = ("y", "zh", "zl")
-REGROUP = ("zl", "zh", "y")
+REGROUP = ("y", "zh", "zl")
 CHUNKS = ("zl", "node", "y")
 PRECISE = lax.Precision.HIGHEST
 F32 = jnp.float32
@@ -57,7 +57,7 @@
     slots = (OWNERS // GROUP) * CAP
     counts = matrix_ref[pl.ds(lax.axis_index(CTX), 1), :].astype(F32)
     nth = lax.shift_right_logical(iota((slots, OWNERS), 0), 4)
-    chunk = (nth & 3) * 4 + lax.shift_right_logical(nth, 2)
+    chunk = nth
     before = iota((slots, OWNERS), 1) < chunk * GROUP
     start = jnp.sum(jnp.where(before, counts, 0.0), axis=1, keepdims=True).astype(jnp.int32)
     wanted = start + (iota((slots, 1), 0) & (CAP - 1))
@@ -101,8 +101,7 @@
     earlier = (iota((OWNERS, OWNERS), 0) < iota((OWNERS, OWNERS), 1)).astype(F32).astype(BF16)
     arrive = dot(counts.astype(BF16), earlier)
     slots = OWNERS * CAP
-    loader = iota((OWNERS, slots), 0)
-    nth = (loader & 3) * 16 + (loader & 12) + lax.shift_right_logical(loader, 4)
+    nth = iota((OWNERS, slots), 0)
     expand = (lax.shift_right_logical(iota((OWNERS, slots), 1), 4) == nth).astype(F32).astype(BF16)
     wide = dot(jnp.concatenate([counts, ends, arrive], axis=0).astype(BF16), expand)
     counts, ends, arrive = wide[:8], wide[8:16], wide[16:]

time: 151 us -> 150 us (level)
  the two profiles are of different devices: /device:TPU:32 before, /device:TPU:6 now
where the time goes in v6:
time: 150 us; the launch traced here: 148 us
  waiting for transfers between devices  72.8 us (49%)
  starting transfers between devices  46.4 us (31%)
  blocking collectives  17.5 us (12%)
  Pallas kernels  11.4 us (8%)
    all_to_all x1, waiting for transfers between devices, local(): lax.all_to_all(packed.reshape(OWNERS, CAP, WIDTH), REGROUP, 0, 0, tiled=T...  64.3 us
    ppermute x4, starting transfers between devices, local(): lax.ppermute(part, ('zh', 'zl'), [(h * 4 + nth, nth * 4 + (h + turn) % 4)...  20.8 us
    all_to_all x1, starting transfers between devices, local(): lax.all_to_all(packed.reshape(OWNERS, CAP, WIDTH), REGROUP, 0, 0, tiled=T...  18.7 us
    all_to_all x1, blocking collectives, local(): maps = lax.all_to_all(maps, CHUNKS, 0, 0, tiled=True)  17.5 us
    all_to_all x1, starting transfers between devices, local(): prefix = lax.all_to_all(prefix, CHUNKS, 0, 0, tiled=True)  6.85 us
    all_to_all x1, waiting for transfers between devices, local(): prefix = lax.all_to_all(prefix, CHUNKS, 0, 0, tiled=True)  5.32 us
    pallas_call x1, Pallas kernels, local(): call(block_kernel, [SMEM, VMEM, VMEM, VMEM], (shape((CHUNK, DV)), shape((...  3.25 us
    ppermute x4, waiting for transfers between devices, local(): lax.ppermute(part, ('zh', 'zl'), [(h * 4 + nth, nth * 4 + (h + turn) % 4)...  3.09 us
  transfers between devices with their start and end apart: 6, of which 4 were waited for; matrix products, arithmetic and copies ran while one was open for 0% of the time, Pallas kernels for 3%

profile of v6, /device:TPU:6, one launch (start us, length us, event | category | flops | bytes accessed | tf_op | source)
XLA Modules:
  0.0 148.2 jit_solution(13807725856542586385)
XLA Ops:
  0.0 3.0 %shard_map.74 = bf16[4,4,4,16,640]{4,3,2,1,0:T(8,128)(2,1)} custom-call(s32[64,64]{1,0:T(8,128)} %bitcast.7, bf16[128,512]{1,0:T(8,128)(2,1)} %bitcast.11, bf16[128,512]{1,0:T(8,128)(2,1)} %bitcast.12, bf16[128,1024]{1,0:T(8,128)(2,1)} %bitcast.10, bf16[128,512]{1,0:T(8,128)(2,1)} %bitcast.13), custom_call_target="tpu_custom_call" | custom-call | flops 268435456 | bytes 1048576 | tf_op jit(solution)/shard_map/pallas_call | solution.py:276
  3.0 0.0 copy-start
  3.0 0.0 copy-start.1
  3.0 18.7 %all-to-all-start = ((bf16[64,16,640]{2,1,0:T(8,128)(2,1)}), bf16[64,16,640]{2,1,0:T(8,128)(2,1)S(1)}, u32[]{:S(2)}, u32[]{:S(2)}) async-start(bf16[64,16,640]{2,1,0:T(8,128)(2,1)} %bitcast.9), calls=%async_computation | async-start | bytes 2621440 | tf_op jit(solution)/shard_map/all_to_all | solution.py:284
  21.7 0.0 copy-done
  21.7 0.9 shard_map.73
  22.6 64.3 %all-to-all-done.received_ref = bf16[64,16,640]{2,1,0:T(8,128)(2,1)S(1)} async-done(((bf16[64,16,640]{2,1,0:T(8,128)(2,1)}), bf16[64,16,640]{2,1,0:T(8,128)(2,1)S(1)}, u32[]{:S(2)}, u32[]{:S(2)}) %all-to-all-start) | async-done | bytes 1310752 | tf_op jit(solution)/shard_map/all_to_all | solution.py:284
  87.0 0.0 copy-done.1
  87.0 0.0 copy-start.2
  87.0 2.1 %shard_map.75 = (bf16[512,512]{1,0:T(8,128)(2,1)S(1)}, f32[64,1,640]{2,1,0:T(1,128)S(1)}) custom-call(s32[8]{0:T(128)S(1)} %copy-done.1, bf16[512,1024]{1,0:T(8,128)(2,1)S(1)} %get-tuple-element.15.pick_ref, bf16[64,16,640]{2,1,0:T(8,128)(2,1)S(1)} %all-to-all-done.received_ref), custom_call_target="tpu_custom_call" | custom-call | flops 536870912 | bytes 1048576 | tf_op jit(solution)/shard_map/pallas_call | solution.py:291
  89.1 17.5 %all_to_all.15.map_ref = f32[64,1,640]{2,1,0:T(1,128)S(1)} all-to-all(f32[64,1,640]{2,1,0:T(1,128)S(1)} %get-tuple-element.16), channel_id=1, replica_groups=mesh['y'=4,'zh'=4,'zl'=4,'node'=4,'tp'=2] {'zl','node','y'}, dimensions={0} | all-to-all | bytes 327680 | tf_op jit(solution)/shard_map/all_to_all | solution.py:297
  106.6 0.8 shard_map.76
  107.4 6.9 %all-to-all-start.2 = ((f32[64,1,512]{2,1,0:T(1,128)}), f32[64,1,512]{2,1,0:T(1,128)S(1)}, u32[]{:S(2)}, u32[]{:S(2)}) async-start(f32[64,1,512]{2,1,0:T(1,128)} %shard_map.76), calls=%async_computation.2 | async-start | bytes 262144 | tf_op jit(solution)/shard_map/all_to_all | solution.py:305
  114.2 0.0 copy-done.2
  114.2 3.2 %shard_map.77 = (f32[512,256]{1,0:T(8,128)S(1)}, f32[512,128]{1,0:T(8,128)S(1)}) custom-call(s32[8]{0:T(128)S(1)} %copy-done.1, s32[1,1024]{1,0:T(1,128)S(1)} %get-tuple-element.17.targets_ref, bf16[64,16,640]{2,1,0:T(8,128)(2,1)S(1)} %all-to-all-done.received_ref, bf16[512,512]{1,0:T(8,128)(2,1)S(1)} %get-tuple-element.18.rows_ref), custom_call_target="tpu_custom_call" | custom-call | flops 1073741824 | bytes 1048576 | tf_op jit(solution)/shard_map/pallas_call | solution.py:298
  117.5 5.3 %all-to-all-done.2.prefix_ref = f32[64,1,512]{2,1,0:T(1,128)S(1)} async-done(((f32[64,1,512]{2,1,0:T(1,128)}), f32[64,1,512]{2,1,0:T(1,128)S(1)}, u32[]{:S(2)}, u32[]{:S(2)}) %all-to-all-start.2) | async-done | bytes 131104 | tf_op jit(solution)/shard_map/all_to_all | solution.py:305
  122.8 0.7 shard_map.78
  123.5 0.7 collective-permute-start
  124.2 4.5 %collective-permute-start.1 = (bf16[128,256]{1,0:T(8,128)(2,1)S(1)}, bf16[128,256]{1,0:T(8,128)(2,1)S(1)}, u32[]{:S(2)}, u32[]{:S(2)}) collective-permute-start(bf16[128,256]{1,0:T(8,128)(2,1)S(1)} %get-tuple-element.22), channel_id=1, source_target_pairs={{0,8},{8,40},{16,72},{24,104},{32,16},{40,48},{48,80},{56,112},{64... | collective-permute-start | bytes 196616 | tf_op jit(solution)/shard_map/ppermute | solution.py:311
  128.7 6.8 %collective-permute-start.2 = (bf16[128,256]{1,0:T(8,128)(2,1)S(1)}, bf16[128,256]{1,0:T(8,128)(2,1)S(1)}, u32[]{:S(2)}, u32[]{:S(2)}) collective-permute-start(bf16[128,256]{1,0:T(8,128)(2,1)S(1)} %get-tuple-element.23), channel_id=1, source_target_pairs={{0,16},{8,48},{16,80},{24,112},{32,24},{40,56},{48,88},{56,120},{6... | collective-permute-start | bytes 196616 | tf_op jit(solution)/shard_map/ppermute | solution.py:311
  135.5 8.8 %collective-permute-start.3 = (bf16[128,256]{1,0:T(8,128)(2,1)S(1)}, bf16[128,256]{1,0:T(8,128)(2,1)S(1)}, u32[]{:S(2)}, u32[]{:S(2)}) collective-permute-start(bf16[128,256]{1,0:T(8,128)(2,1)S(1)} %get-tuple-element.24), channel_id=1, source_target_pairs={{0,24},{8,56},{16,88},{24,120},{32,0},{40,32},{48,64},{56,96},{64,... | collective-permute-start | bytes 196616 | tf_op jit(solution)/shard_map/ppermute | solution.py:311
  144.4 0.0 collective-permute-done.refs_0_
  144.4 0.0 collective-permute-done.1.refs_1_
  144.4 0.5 collective-permute-done.2.refs_2_
  144.9 2.6 %collective-permute-done.3.refs_3_ = bf16[128,256]{1,0:T(8,128)(2,1)S(1)} collective-permute-done((bf16[128,256]{1,0:T(8,128)(2,1)S(1)}, bf16[128,256]{1,0:T(8,128)(2,1)S(1)}, u32[]{:S(2)}, u32[]{:S(2)}) %collective-permute-start.3) | collective-permute-done | bytes 65568 | tf_op jit(solution)/shard_map/ppermute | solution.py:311
  147.5 0.7 shard_map.79
  (1 shorter events, 0.0 us)
Async XLA Ops:
  3.0 18.8 %copy-start = (s32[1,64,64]{2,1,0:T(8,128)S(1)}, s32[1,64,64]{2,1,0:T(8,128)}, u32[]{:S(2)}) copy-start(s32[1,64,64]{2,1,0:T(8,128)} %param.11) | copy-start | bytes 49156
  3.0 84.0 %copy-start.1 = (s32[8]{0:T(128)S(1)}, s32[8]{0:T(128)}, u32[]{:S(2)}) copy-start(s32[8]{0:T(128)} %lengths_ref.3) | copy-start | bytes 100
  3.0 84.0 %all-to-all-start = ((bf16[64,16,640]{2,1,0:T(8,128)(2,1)}), bf16[64,16,640]{2,1,0:T(8,128)(2,1)S(1)}, u32[]{:S(2)}, u32[]{:S(2)}) async-start(bf16[64,16,640]{2,1,0:T(8,128)(2,1)} %bitcast.9), calls=%async_computation | async-start | bytes 2621440 | tf_op jit(solution)/shard_map/all_to_all | solution.py:284
  87.0 27.3 %copy-start.2 = (f32[1024]{0:T(1024)S(1)}, f32[1024]{0:T(1024)}, u32[]{:S(2)}) copy-start(f32[1024]{0:T(1024)} %param.13) | copy-start | bytes 12292
  107.4 15.5 %all-to-all-start.2 = ((f32[64,1,512]{2,1,0:T(1,128)}), f32[64,1,512]{2,1,0:T(1,128)S(1)}, u32[]{:S(2)}, u32[]{:S(2)}) async-start(f32[64,1,512]{2,1,0:T(1,128)} %shard_map.76), calls=%async_computation.2 | async-start | bytes 262144 | tf_op jit(solution)/shard_map/all_to_all | solution.py:305
  123.5 20.8 %collective-permute-start = (bf16[128,256]{1,0:T(8,128)(2,1)S(1)}, bf16[128,256]{1,0:T(8,128)(2,1)S(1)}, u32[]{:S(2)}, u32[]{:S(2)}) collective-permute-start(bf16[128,256]{1,0:T(8,128)(2,1)S(1)} %get-tuple-element.21), channel_id=1, source_target_pairs={{0,0},{8,32},{16,64},{24,96},{32,8},{40,40},{48,72},{56,104},{64,1... | collective-permute-start | bytes 196616 | tf_op jit(solution)/shard_map/ppermute | solution.py:311
  124.2 20.2 %collective-permute-start.1 = (bf16[128,256]{1,0:T(8,128)(2,1)S(1)}, bf16[128,256]{1,0:T(8,128)(2,1)S(1)}, u32[]{:S(2)}, u32[]{:S(2)}) collective-permute-start(bf16[128,256]{1,0:T(8,128)(2,1)S(1)} %get-tuple-element.22), channel_id=1, source_target_pairs={{0,8},{8,40},{16,72},{24,104},{32,16},{40,48},{48,80},{56,112},{64... | collective-permute-start | bytes 196616 | tf_op jit(solution)/shard_map/ppermute | solution.py:311
  128.7 16.2 %collective-permute-start.2 = (bf16[128,256]{1,0:T(8,128)(2,1)S(1)}, bf16[128,256]{1,0:T(8,128)(2,1)S(1)}, u32[]{:S(2)}, u32[]{:S(2)}) collective-permute-start(bf16[128,256]{1,0:T(8,128)(2,1)S(1)} %get-tuple-element.23), channel_id=1, source_target_pairs={{0,16},{8,48},{16,80},{24,112},{32,24},{40,56},{48,88},{56,120},{6... | collective-permute-start | bytes 196616 | tf_op jit(solution)/shard_map/ppermute | solution.py:311
  135.5 11.9 %collective-permute-start.3 = (bf16[128,256]{1,0:T(8,128)(2,1)S(1)}, bf16[128,256]{1,0:T(8,128)(2,1)S(1)}, u32[]{:S(2)}, u32[]{:S(2)}) collective-permute-start(bf16[128,256]{1,0:T(8,128)(2,1)S(1)} %get-tuple-element.24), channel_id=1, source_target_pairs={{0,24},{8,56},{16,88},{24,120},{32,0},{40,32},{48,64},{56,96},{64,... | collective-permute-start | bytes 196616 | tf_op jit(solution)/shard_map/ppermute | solution.py:311

commit v7 on v6

--- a/solution.py
+++ b/solution.py
@@ -7,6 +7,7 @@
 
 DK = 128
 DV = 256
+TURN = (3, 0, 2, 1)
 HEADS = 4
 GROUP = 4
 TOK = 128
@@ -45,8 +46,8 @@
 
 
 def pack_kernel(
-    matrix_hbm, query_hbm, key_hbm, value_hbm, rate_hbm, out_ref,
-    matrix_ref, query_ref, key_ref, value_ref, rate_ref, sems,
+    matrix_hbm, query_hbm, key_hbm, value_hbm, rate_hbm, out_hbm,
+    matrix_ref, query_ref, key_ref, value_ref, rate_ref, out_ref, sems, out_sems,
 ):
     sources = (matrix_hbm, key_hbm, rate_hbm, value_hbm, query_hbm)
     targets = (matrix_ref, key_ref, rate_ref, value_ref, query_ref)
@@ -63,17 +64,33 @@
     wanted = start + (iota((slots, 1), 0) & (CAP - 1))
     pick = (iota((slots, TOK), 1) == wanted).astype(F32).astype(BF16)
     at = 0
+    leaving = []
     for copy, ref, width in zip(copies[1:], targets[1:], (DK, DK, DV, DK)):
         copy.wait()
         rows = dot(pick, ref[...]).astype(BF16)
         for head in range(HEADS):
             piece = rows[:, head * width : (head + 1) * width]
-            out_ref[:, head, :, :, at : at + width] = piece.reshape(4, 4, CAP, width)
+            piece = piece.reshape(4, 4, CAP, width)
+            for nth, turn in enumerate(TURN):
+                out_ref[:, head, nth, :, at : at + width] = piece[:, (head + turn) % 4]
+        columns = pl.ds(at, width)
+        leaving.append(
+            pltpu.make_async_copy(
+                out_ref.at[:, :, :, :, columns],
+                out_hbm.at[:, :, :, :, columns],
+                out_sems.at[len(leaving)],
+            )
+        )
+        leaving[-1].start()
         at += width
+    for copy in leaving:
+        copy.wait()
 
 
 def chunk_in_group():
-    return lax.axis_index("y") * 4 + lax.axis_index("zl")
+    nth = lax.axis_index("zl")
+    turn = sum([jnp.where(nth == i, turn, 0) for i, turn in enumerate(TURN)])
+    return lax.axis_index("y") * 4 + ((lax.axis_index("zh") + turn) & 3)
 
 
 def chunk_start():
@@ -212,9 +229,12 @@
     state = jnp.zeros((rows, 2 * DV), F32)
     kept = jnp.ones((rows, 2 * DV), F32)
     inside = []
-    for nth in range(GROUP):
-        inside.append((kept, state))
-        here = map_ref[nth * rows : (nth + 1) * rows, 0, :]
+    for chunk in range(GROUP):
+        turn = (chunk - lax.axis_index("zh")) & 3
+        nth = sum([jnp.where(turn == a, i, 0) for i, a in enumerate(TURN)])
+        span = pl.ds(nth * rows, rows)
+        inside.append((span, kept, state))
+        here = map_ref[span, 0, :]
         own = here[:, 2 * DV :]
         other = pltpu.roll(own, DK // 2, 1)
         one, two = jnp.where(low, own, other), jnp.where(low, other, own)
@@ -228,8 +248,8 @@
         kept = kept * jnp.where(row < step, 1.0, pltpu.roll(kept, step, 0))
         step *= 2
     before = jnp.where(row < 1, 0.0, pltpu.roll(state, 1, 0))
-    for nth, (kept, state) in enumerate(inside):
-        prefix_ref[nth * rows : (nth + 1) * rows, 0, :] = kept * before + state
+    for span, kept, state in inside:
+        prefix_ref[span, 0, :] = kept * before + state
 
 
 def finish_kernel(prefix_ref, partial_ref, query_ref, gain_ref, *out_refs):
@@ -237,7 +257,7 @@
     head = lax.axis_index("zh")
     gain = gain_ref[pl.ds(head, 1), :]
     for turn, out_ref in enumerate(out_refs):
-        span = pl.ds(pl.multiple_of(((head + turn) & 3) * TOK, TOK), TOK)
+        span = pl.ds(pl.multiple_of((head ^ turn) * TOK, TOK), TOK)
         mixed = partial_ref[span, :] + dot(query_ref[span, :], state, precision=PRECISE)
         scale = lax.rsqrt(jnp.mean(mixed * mixed, axis=1, keepdims=True) + EPSILON)
         out_ref[...] = (mixed * scale * gain).astype(BF16)
@@ -245,7 +265,7 @@
 
 def join_kernel(*refs):
     for turn, ref in enumerate(refs[:-1]):
-        head = (lax.axis_index("zl") - turn) & 3
+        head = lax.axis_index("zl") ^ turn
         refs[-1][:, pl.ds(pl.multiple_of(head * DV, DV), DV)] = ref[...]
 
 
@@ -254,12 +274,12 @@
 HBM = pl.BlockSpec(memory_space=pltpu.HBM)
 
 
-def call(kernel, specs, outs, cost=0, scratch=(), limit=32 << 20):
+def call(kernel, specs, outs, cost=0, scratch=(), limit=32 << 20, out_spec=None):
     return pl.pallas_call(
         kernel,
         out_shape=outs,
         in_specs=specs,
-        out_specs=jax.tree.map(lambda _: VMEM, outs),
+        out_specs=jax.tree.map(lambda _: out_spec or VMEM, outs),
         scratch_shapes=scratch,
         compiler_params=pltpu.CompilerParams(vmem_limit_bytes=limit),
         cost_estimate=pl.CostEstimate(flops=cost, bytes_accessed=1 << 20, transcendentals=0),
@@ -278,8 +298,11 @@
         [HBM] * 5,
         shape((4, HEADS, 4, CAP, WIDTH), BF16),
         1 << 28,
-        [pltpu.VMEM(a.shape, a.dtype) for a in streams] + [pltpu.SemaphoreType.DMA((5,))],
+        [pltpu.VMEM(a.shape, a.dtype) for a in streams]
+        + [pltpu.VMEM((4, HEADS, 4, CAP, WIDTH), BF16)]
+        + [pltpu.SemaphoreType.DMA((5,)), pltpu.SemaphoreType.DMA((4,))],
         65500000,
+        HBM,
     )(*streams)
     received = lax.all_to_all(packed.reshape(OWNERS, CAP, WIDTH), REGROUP, 0, 0, tiled=True)
     targets, pick = call(
@@ -309,7 +332,7 @@
     pairs = [(head, nth) for head in range(HEADS) for nth in range(GROUP)]
     parts = [
         lax.ppermute(
-            part, ("zh", "zl"), [(h * 4 + nth, nth * 4 + (h + turn) % 4) for h, nth in pairs]
+            part, ("zh", "zl"), [(h * 4 + n, (h + TURN[n]) % 4 * 4 + (h ^ turn)) for h, n in pairs]
         )
         for turn, part in enumerate(parts)
     ]

time: 150 us -> 149 us (level)
  starting transfers between devices: 46.4 us -> 43.9 us
  waiting for transfers between devices: 72.8 us -> 75.2 us
    ppermute x4, waiting for transfers between devices: 3.09 us -> 5.58 us  [local(): lax.ppermute(part, ('zh', 'zl'), [(h * 4 + n, (h + TURN[n]) % 4 * 4 + (h...]
    ppermute x4, starting transfers between devices: 20.8 us -> 18.3 us  [local(): lax.ppermute(part, ('zh', 'zl'), [(h * 4 + n, (h + TURN[n]) % 4 * 4 + (h...]
where the time goes in v7:
time: 149 us; the launch traced here: 148 us
  waiting for transfers between devices  75.2 us (50%)
  starting transfers between devices  43.9 us (29%)
  blocking collectives  17.5 us (12%)
  Pallas kernels  11.1 us (7%)
    all_to_all x1, waiting for transfers between devices, local(): lax.all_to_all(packed.reshape(OWNERS, CAP, WIDTH), REGROUP, 0, 0, tiled=T...  64.3 us
    all_to_all x1, starting transfers between devices, local(): lax.all_to_all(packed.reshape(OWNERS, CAP, WIDTH), REGROUP, 0, 0, tiled=T...  18.7 us
    ppermute x4, starting transfers between devices, local(): lax.ppermute(part, ('zh', 'zl'), [(h * 4 + n, (h + TURN[n]) % 4 * 4 + (h...  18.3 us
    all_to_all x1, blocking collectives, local(): maps = lax.all_to_all(maps, CHUNKS, 0, 0, tiled=True)  17.5 us
    all_to_all x1, starting transfers between devices, local(): prefix = lax.all_to_all(prefix, CHUNKS, 0, 0, tiled=True)  6.85 us
    ppermute x4, waiting for transfers between devices, local(): lax.ppermute(part, ('zh', 'zl'), [(h * 4 + n, (h + TURN[n]) % 4 * 4 + (h...  5.58 us
    all_to_all x1, waiting for transfers between devices, local(): prefix = lax.all_to_all(prefix, CHUNKS, 0, 0, tiled=True)  5.32 us
    pallas_call x1, Pallas kernels, local(): call(block_kernel, [SMEM, VMEM, VMEM, VMEM], (shape((CHUNK, DV)), shape((...  3.25 us
  transfers between devices with their start and end apart: 6, of which 4 were waited for; matrix products, arithmetic and copies ran while one was open for 0% of the time, Pallas kernels for 3%

profile of v7, /device:TPU:6, one launch (start us, length us, event | category | flops | bytes accessed | tf_op | source)
XLA Modules:
  0.0 147.9 jit_solution(9498866676276254812)
XLA Ops:
  0.0 2.6 %shard_map.74 = bf16[4,4,4,16,640]{4,3,2,1,0:T(8,128)(2,1)} custom-call(s32[64,64]{1,0:T(8,128)} %bitcast.7, bf16[128,512]{1,0:T(8,128)(2,1)} %bitcast.11, bf16[128,512]{1,0:T(8,128)(2,1)} %bitcast.12, bf16[128,1024]{1,0:T(8,128)(2,1)} %bitcast.10, bf16[128,512]{1,0:T(8,128)(2,1)} %bitcast.13), custom_call_target="tpu_custom_call" | custom-call | flops 268435456 | bytes 1048576 | tf_op jit(solution)/shard_map/pallas_call | solution.py:296
  2.7 0.0 copy-start
  2.7 0.0 copy-start.1
  2.7 18.7 %all-to-all-start = ((bf16[64,16,640]{2,1,0:T(8,128)(2,1)}), bf16[64,16,640]{2,1,0:T(8,128)(2,1)S(1)}, u32[]{:S(2)}, u32[]{:S(2)}) async-start(bf16[64,16,640]{2,1,0:T(8,128)(2,1)} %bitcast.9), calls=%async_computation | async-start | bytes 2621440 | tf_op jit(solution)/shard_map/all_to_all | solution.py:307
  21.4 0.0 copy-done
  21.4 0.9 shard_map.73
  22.3 64.3 %all-to-all-done.received_ref = bf16[64,16,640]{2,1,0:T(8,128)(2,1)S(1)} async-done(((bf16[64,16,640]{2,1,0:T(8,128)(2,1)}), bf16[64,16,640]{2,1,0:T(8,128)(2,1)S(1)}, u32[]{:S(2)}, u32[]{:S(2)}) %all-to-all-start) | async-done | bytes 1310752 | tf_op jit(solution)/shard_map/all_to_all | solution.py:307
  86.6 0.0 copy-done.1
  86.6 0.0 copy-start.2
  86.7 2.1 %shard_map.75 = (bf16[512,512]{1,0:T(8,128)(2,1)S(1)}, f32[64,1,640]{2,1,0:T(1,128)S(1)}) custom-call(s32[8]{0:T(128)S(1)} %copy-done.1, bf16[512,1024]{1,0:T(8,128)(2,1)S(1)} %get-tuple-element.15.pick_ref, bf16[64,16,640]{2,1,0:T(8,128)(2,1)S(1)} %all-to-all-done.received_ref), custom_call_target="tpu_custom_call" | custom-call | flops 536870912 | bytes 1048576 | tf_op jit(solution)/shard_map/pallas_call | solution.py:314
  88.8 17.5 %all_to_all.15.map_ref = f32[64,1,640]{2,1,0:T(1,128)S(1)} all-to-all(f32[64,1,640]{2,1,0:T(1,128)S(1)} %get-tuple-element.16), channel_id=1, replica_groups=mesh['y'=4,'zh'=4,'zl'=4,'node'=4,'tp'=2] {'zl','node','y'}, dimensions={0} | all-to-all | bytes 327680 | tf_op jit(solution)/shard_map/all_to_all | solution.py:320
  106.2 0.8 shard_map.76
  107.1 6.9 %all-to-all-start.2 = ((f32[64,1,512]{2,1,0:T(1,128)}), f32[64,1,512]{2,1,0:T(1,128)S(1)}, u32[]{:S(2)}, u32[]{:S(2)}) async-start(f32[64,1,512]{2,1,0:T(1,128)} %shard_map.76), calls=%async_computation.2 | async-start | bytes 262144 | tf_op jit(solution)/shard_map/all_to_all | solution.py:328
  113.9 0.0 copy-done.2
  113.9 3.2 %shard_map.77 = (f32[512,256]{1,0:T(8,128)S(1)}, f32[512,128]{1,0:T(8,128)S(1)}) custom-call(s32[8]{0:T(128)S(1)} %copy-done.1, s32[1,1024]{1,0:T(1,128)S(1)} %get-tuple-element.17.targets_ref, bf16[64,16,640]{2,1,0:T(8,128)(2,1)S(1)} %all-to-all-done.received_ref, bf16[512,512]{1,0:T(8,128)(2,1)S(1)} %get-tuple-element.18.rows_ref), custom_call_target="tpu_custom_call" | custom-call | flops 1073741824 | bytes 1048576 | tf_op jit(solution)/shard_map/pallas_call | solution.py:321
  117.2 5.3 %all-to-all-done.2.prefix_ref = f32[64,1,512]{2,1,0:T(1,128)S(1)} async-done(((f32[64,1,512]{2,1,0:T(1,128)}), f32[64,1,512]{2,1,0:T(1,128)S(1)}, u32[]{:S(2)}, u32[]{:S(2)}) %all-to-all-start.2) | async-done | bytes 131104 | tf_op jit(solution)/shard_map/all_to_all | solution.py:328
  122.5 0.7 shard_map.78
  123.2 3.6 %collective-permute-start = (bf16[128,256]{1,0:T(8,128)(2,1)S(1)}, bf16[128,256]{1,0:T(8,128)(2,1)S(1)}, u32[]{:S(2)}, u32[]{:S(2)}) collective-permute-start(bf16[128,256]{1,0:T(8,128)(2,1)S(1)} %get-tuple-element.21), channel_id=1, source_target_pairs={{0,96},{8,0},{16,64},{24,32},{32,8},{40,40},{48,104},{56,72},{64,4... | collective-permute-start | bytes 196616 | tf_op jit(solution)/shard_map/ppermute | solution.py:334
  126.8 2.0 %collective-permute-start.1 = (bf16[128,256]{1,0:T(8,128)(2,1)S(1)}, bf16[128,256]{1,0:T(8,128)(2,1)S(1)}, u32[]{:S(2)}, u32[]{:S(2)}) collective-permute-start(bf16[128,256]{1,0:T(8,128)(2,1)S(1)} %get-tuple-element.22), channel_id=1, source_target_pairs={{0,104},{8,8},{16,72},{24,40},{32,0},{40,32},{48,96},{56,64},{64,5... | collective-permute-start | bytes 196616 | tf_op jit(solution)/shard_map/ppermute | solution.py:334
  128.7 10.9 %collective-permute-start.2 = (bf16[128,256]{1,0:T(8,128)(2,1)S(1)}, bf16[128,256]{1,0:T(8,128)(2,1)S(1)}, u32[]{:S(2)}, u32[]{:S(2)}) collective-permute-start(bf16[128,256]{1,0:T(8,128)(2,1)S(1)} %get-tuple-element.23), channel_id=1, source_target_pairs={{0,112},{8,16},{16,80},{24,48},{32,24},{40,56},{48,120},{56,88},{6... | collective-permute-start | bytes 196616 | tf_op jit(solution)/shard_map/ppermute | solution.py:334
  139.7 1.9 %collective-permute-start.3 = (bf16[128,256]{1,0:T(8,128)(2,1)S(1)}, bf16[128,256]{1,0:T(8,128)(2,1)S(1)}, u32[]{:S(2)}, u32[]{:S(2)}) collective-permute-start(bf16[128,256]{1,0:T(8,128)(2,1)S(1)} %get-tuple-element.24), channel_id=1, source_target_pairs={{0,120},{8,24},{16,88},{24,56},{32,16},{40,48},{48,112},{56,80},{6... | collective-permute-start | bytes 196616 | tf_op jit(solution)/shard_map/ppermute | solution.py:334
  141.6 0.0 collective-permute-done.refs_0_
  141.6 0.0 collective-permute-done.1.refs_1_
  141.6 0.7 collective-permute-done.2.refs_2_
  142.3 4.9 %collective-permute-done.3.refs_3_ = bf16[128,256]{1,0:T(8,128)(2,1)S(1)} collective-permute-done((bf16[128,256]{1,0:T(8,128)(2,1)S(1)}, bf16[128,256]{1,0:T(8,128)(2,1)S(1)}, u32[]{:S(2)}, u32[]{:S(2)}) %collective-permute-start.3) | collective-permute-done | bytes 65568 | tf_op jit(solution)/shard_map/ppermute | solution.py:334
  147.2 0.7 shard_map.79
  (1 shorter events, 0.0 us)
Async XLA Ops:
  2.7 18.8 %copy-start = (s32[1,64,64]{2,1,0:T(8,128)S(1)}, s32[1,64,64]{2,1,0:T(8,128)}, u32[]{:S(2)}) copy-start(s32[1,64,64]{2,1,0:T(8,128)} %param.11) | copy-start | bytes 49156
  2.7 84.0 %copy-start.1 = (s32[8]{0:T(128)S(1)}, s32[8]{0:T(128)}, u32[]{:S(2)}) copy-start(s32[8]{0:T(128)} %lengths_ref.3) | copy-start | bytes 100
  2.7 84.0 %all-to-all-start = ((bf16[64,16,640]{2,1,0:T(8,128)(2,1)}), bf16[64,16,640]{2,1,0:T(8,128)(2,1)S(1)}, u32[]{:S(2)}, u32[]{:S(2)}) async-start(bf16[64,16,640]{2,1,0:T(8,128)(2,1)} %bitcast.9), calls=%async_computation | async-start | bytes 2621440 | tf_op jit(solution)/shard_map/all_to_all | solution.py:307
  86.6 27.3 %copy-start.2 = (f32[1024]{0:T(1024)S(1)}, f32[1024]{0:T(1024)}, u32[]{:S(2)}) copy-start(f32[1024]{0:T(1024)} %param.13) | copy-start | bytes 12292
  107.1 15.5 %all-to-all-start.2 = ((f32[64,1,512]{2,1,0:T(1,128)}), f32[64,1,512]{2,1,0:T(1,128)S(1)}, u32[]{:S(2)}, u32[]{:S(2)}) async-start(f32[64,1,512]{2,1,0:T(1,128)} %shard_map.76), calls=%async_computation.2 | async-start | bytes 262144 | tf_op jit(solution)/shard_map/all_to_all | solution.py:328
  123.2 18.4 %collective-permute-start = (bf16[128,256]{1,0:T(8,128)(2,1)S(1)}, bf16[128,256]{1,0:T(8,128)(2,1)S(1)}, u32[]{:S(2)}, u32[]{:S(2)}) collective-permute-start(bf16[128,256]{1,0:T(8,128)(2,1)S(1)} %get-tuple-element.21), channel_id=1, source_target_pairs={{0,96},{8,0},{16,64},{24,32},{32,8},{40,40},{48,104},{56,72},{64,4... | collective-permute-start | bytes 196616 | tf_op jit(solution)/shard_map/ppermute | solution.py:334
  126.8 14.8 %collective-permute-start.1 = (bf16[128,256]{1,0:T(8,128)(2,1)S(1)}, bf16[128,256]{1,0:T(8,128)(2,1)S(1)}, u32[]{:S(2)}, u32[]{:S(2)}) collective-permute-start(bf16[128,256]{1,0:T(8,128)(2,1)S(1)} %get-tuple-element.22), channel_id=1, source_target_pairs={{0,104},{8,8},{16,72},{24,40},{32,0},{40,32},{48,96},{56,64},{64,5... | collective-permute-start | bytes 196616 | tf_op jit(solution)/shard_map/ppermute | solution.py:334
  128.7 13.6 %collective-permute-start.2 = (bf16[128,256]{1,0:T(8,128)(2,1)S(1)}, bf16[128,256]{1,0:T(8,128)(2,1)S(1)}, u32[]{:S(2)}, u32[]{:S(2)}) collective-permute-start(bf16[128,256]{1,0:T(8,128)(2,1)S(1)} %get-tuple-element.23), channel_id=1, source_target_pairs={{0,112},{8,16},{16,80},{24,48},{32,24},{40,56},{48,120},{56,88},{6... | collective-permute-start | bytes 196616 | tf_op jit(solution)/shard_map/ppermute | solution.py:334
  139.7 7.5 %collective-permute-start.3 = (bf16[128,256]{1,0:T(8,128)(2,1)S(1)}, bf16[128,256]{1,0:T(8,128)(2,1)S(1)}, u32[]{:S(2)}, u32[]{:S(2)}) collective-permute-start(bf16[128,256]{1,0:T(8,128)(2,1)S(1)} %get-tuple-element.24), channel_id=1, source_target_pairs={{0,120},{8,24},{16,88},{24,56},{32,16},{40,48},{48,112},{56,80},{6... | collective-permute-start | bytes 196616 | tf_op jit(solution)/shard_map/ppermute | solution.py:334

commit v8 on v7

--- a/solution.py
+++ b/solution.py
@@ -19,7 +19,7 @@
 EPSILON = 1e-05
 CTX = ("y", "zh", "zl")
 REGROUP = ("y", "zh", "zl")
-CHUNKS = ("zl", "node", "y")
+CHUNKS = ("node", "zl", "y")
 PRECISE = lax.Precision.HIGHEST
 F32 = jnp.float32
 BF16 = jnp.bfloat16
@@ -232,9 +232,9 @@
     for chunk in range(GROUP):
         turn = (chunk - lax.axis_index("zh")) & 3
         nth = sum([jnp.where(turn == a, i, 0) for i, a in enumerate(TURN)])
-        span = pl.ds(nth * rows, rows)
-        inside.append((span, kept, state))
-        here = map_ref[span, 0, :]
+        spans = [pl.ds(node * 16 + nth * 4, 4) for node in range(rows // 4)]
+        inside.append((spans, kept, state))
+        here = jnp.concatenate([map_ref[span, 0, :] for span in spans], axis=0)
         own = here[:, 2 * DV :]
         other = pltpu.roll(own, DK // 2, 1)
         one, two = jnp.where(low, own, other), jnp.where(low, other, own)
@@ -248,8 +248,10 @@
         kept = kept * jnp.where(row < step, 1.0, pltpu.roll(kept, step, 0))
         step *= 2
     before = jnp.where(row < 1, 0.0, pltpu.roll(state, 1, 0))
-    for span, kept, state in inside:
-        prefix_ref[span, 0, :] = kept * before + state
+    for spans, kept, state in inside:
+        out = kept * before + state
+        for node, span in enumerate(spans):
+            prefix_ref[span, 0, :] = out[4 * node : 4 * node + 4]
 
 
 def finish_kernel(prefix_ref, partial_ref, query_ref, gain_ref, *out_refs):

time: 149 us -> 149 us (level)
  no operation moved by 1% of the time
where the time goes in v8:
time: 149 us; the launch traced here: 148 us
  waiting for transfers between devices  75.3 us (51%)
  starting transfers between devices  43.1 us (29%)
  blocking collectives  17.9 us (12%)
  Pallas kernels  11.1 us (7%)
    all_to_all x1, waiting for transfers between devices, local(): lax.all_to_all(packed.reshape(OWNERS, CAP, WIDTH), REGROUP, 0, 0, tiled=T...  64.3 us
    all_to_all x1, starting transfers between devices, local(): lax.all_to_all(packed.reshape(OWNERS, CAP, WIDTH), REGROUP, 0, 0, tiled=T...  18.7 us
    all_to_all x1, blocking collectives, local(): maps = lax.all_to_all(maps, CHUNKS, 0, 0, tiled=True)  17.9 us
    ppermute x4, starting transfers between devices, local(): lax.ppermute(part, ('zh', 'zl'), [(h * 4 + n, (h + TURN[n]) % 4 * 4 + (h...  17.8 us
    all_to_all x1, starting transfers between devices, local(): prefix = lax.all_to_all(prefix, CHUNKS, 0, 0, tiled=True)  6.55 us
    all_to_all x1, waiting for transfers between devices, local(): prefix = lax.all_to_all(prefix, CHUNKS, 0, 0, tiled=True)  5.49 us
    ppermute x4, waiting for transfers between devices, local(): lax.ppermute(part, ('zh', 'zl'), [(h * 4 + n, (h + TURN[n]) % 4 * 4 + (h...  5.43 us
    pallas_call x1, Pallas kernels, local(): call(block_kernel, [SMEM, VMEM, VMEM, VMEM], (shape((CHUNK, DV)), shape((...  3.25 us
  transfers between devices with their start and end apart: 6, of which 4 were waited for; matrix products, arithmetic and copies ran while one was open for 0% of the time, Pallas kernels for 3%

profile of v8, /device:TPU:6, one launch (start us, length us, event | category | flops | bytes accessed | tf_op | source)
XLA Modules:
  0.0 147.5 jit_solution(14903727878955613392)
XLA Ops:
  0.0 2.6 %shard_map.74 = bf16[4,4,4,16,640]{4,3,2,1,0:T(8,128)(2,1)} custom-call(s32[64,64]{1,0:T(8,128)} %bitcast.7, bf16[128,512]{1,0:T(8,128)(2,1)} %bitcast.11, bf16[128,512]{1,0:T(8,128)(2,1)} %bitcast.12, bf16[128,1024]{1,0:T(8,128)(2,1)} %bitcast.10, bf16[128,512]{1,0:T(8,128)(2,1)} %bitcast.13), custom_call_target="tpu_custom_call" | custom-call | flops 268435456 | bytes 1048576 | tf_op jit(solution)/shard_map/pallas_call | solution.py:298
  2.7 0.0 copy-start
  2.7 0.0 copy-start.1
  2.7 18.7 %all-to-all-start = ((bf16[64,16,640]{2,1,0:T(8,128)(2,1)}), bf16[64,16,640]{2,1,0:T(8,128)(2,1)S(1)}, u32[]{:S(2)}, u32[]{:S(2)}) async-start(bf16[64,16,640]{2,1,0:T(8,128)(2,1)} %bitcast.9), calls=%async_computation | async-start | bytes 2621440 | tf_op jit(solution)/shard_map/all_to_all | solution.py:309
  21.4 0.0 copy-done
  21.4 0.9 shard_map.73
  22.3 64.3 %all-to-all-done.received_ref = bf16[64,16,640]{2,1,0:T(8,128)(2,1)S(1)} async-done(((bf16[64,16,640]{2,1,0:T(8,128)(2,1)}), bf16[64,16,640]{2,1,0:T(8,128)(2,1)S(1)}, u32[]{:S(2)}, u32[]{:S(2)}) %all-to-all-start) | async-done | bytes 1310752 | tf_op jit(solution)/shard_map/all_to_all | solution.py:309
  86.6 0.0 copy-done.1
  86.6 0.0 copy-start.2
  86.7 2.1 %shard_map.75 = (bf16[512,512]{1,0:T(8,128)(2,1)S(1)}, f32[64,1,640]{2,1,0:T(1,128)S(1)}) custom-call(s32[8]{0:T(128)S(1)} %copy-done.1, bf16[512,1024]{1,0:T(8,128)(2,1)S(1)} %get-tuple-element.15.pick_ref, bf16[64,16,640]{2,1,0:T(8,128)(2,1)S(1)} %all-to-all-done.received_ref), custom_call_target="tpu_custom_call" | custom-call | flops 536870912 | bytes 1048576 | tf_op jit(solution)/shard_map/pallas_call | solution.py:316
  88.8 17.9 %all_to_all.15.map_ref = f32[64,1,640]{2,1,0:T(1,128)S(1)} all-to-all(f32[64,1,640]{2,1,0:T(1,128)S(1)} %get-tuple-element.16), channel_id=1, replica_groups=mesh['y'=4,'zh'=4,'zl'=4,'node'=4,'tp'=2] {'node','zl','y'}, dimensions={0} | all-to-all | bytes 327680 | tf_op jit(solution)/shard_map/all_to_all | solution.py:322
  106.7 0.8 shard_map.76
  107.5 6.5 %all-to-all-start.2 = ((f32[64,1,512]{2,1,0:T(1,128)}), f32[64,1,512]{2,1,0:T(1,128)S(1)}, u32[]{:S(2)}, u32[]{:S(2)}) async-start(f32[64,1,512]{2,1,0:T(1,128)} %shard_map.76), calls=%async_computation.2 | async-start | bytes 262144 | tf_op jit(solution)/shard_map/all_to_all | solution.py:330
  114.0 0.0 copy-done.2
  114.1 3.2 %shard_map.77 = (f32[512,256]{1,0:T(8,128)S(1)}, f32[512,128]{1,0:T(8,128)S(1)}) custom-call(s32[8]{0:T(128)S(1)} %copy-done.1, s32[1,1024]{1,0:T(1,128)S(1)} %get-tuple-element.17.targets_ref, bf16[64,16,640]{2,1,0:T(8,128)(2,1)S(1)} %all-to-all-done.received_ref, bf16[512,512]{1,0:T(8,128)(2,1)S(1)} %get-tuple-element.18.rows_ref), custom_call_target="tpu_custom_call" | custom-call | flops 1073741824 | bytes 1048576 | tf_op jit(solution)/shard_map/pallas_call | solution.py:323
  117.3 5.5 %all-to-all-done.2.prefix_ref = f32[64,1,512]{2,1,0:T(1,128)S(1)} async-done(((f32[64,1,512]{2,1,0:T(1,128)}), f32[64,1,512]{2,1,0:T(1,128)S(1)}, u32[]{:S(2)}, u32[]{:S(2)}) %all-to-all-start.2) | async-done | bytes 131104 | tf_op jit(solution)/shard_map/all_to_all | solution.py:330
  122.8 0.7 shard_map.78
  123.5 3.6 %collective-permute-start = (bf16[128,256]{1,0:T(8,128)(2,1)S(1)}, bf16[128,256]{1,0:T(8,128)(2,1)S(1)}, u32[]{:S(2)}, u32[]{:S(2)}) collective-permute-start(bf16[128,256]{1,0:T(8,128)(2,1)S(1)} %get-tuple-element.21), channel_id=1, source_target_pairs={{0,96},{8,0},{16,64},{24,32},{32,8},{40,40},{48,104},{56,72},{64,4... | collective-permute-start | bytes 196616 | tf_op jit(solution)/shard_map/ppermute | solution.py:336
  127.1 1.9 %collective-permute-start.1 = (bf16[128,256]{1,0:T(8,128)(2,1)S(1)}, bf16[128,256]{1,0:T(8,128)(2,1)S(1)}, u32[]{:S(2)}, u32[]{:S(2)}) collective-permute-start(bf16[128,256]{1,0:T(8,128)(2,1)S(1)} %get-tuple-element.22), channel_id=1, source_target_pairs={{0,104},{8,8},{16,72},{24,40},{32,0},{40,32},{48,96},{56,64},{64,5... | collective-permute-start | bytes 196616 | tf_op jit(solution)/shard_map/ppermute | solution.py:336
  129.0 10.4 %collective-permute-start.2 = (bf16[128,256]{1,0:T(8,128)(2,1)S(1)}, bf16[128,256]{1,0:T(8,128)(2,1)S(1)}, u32[]{:S(2)}, u32[]{:S(2)}) collective-permute-start(bf16[128,256]{1,0:T(8,128)(2,1)S(1)} %get-tuple-element.23), channel_id=1, source_target_pairs={{0,112},{8,16},{16,80},{24,48},{32,24},{40,56},{48,120},{56,88},{6... | collective-permute-start | bytes 196616 | tf_op jit(solution)/shard_map/ppermute | solution.py:336
  139.4 1.9 %collective-permute-start.3 = (bf16[128,256]{1,0:T(8,128)(2,1)S(1)}, bf16[128,256]{1,0:T(8,128)(2,1)S(1)}, u32[]{:S(2)}, u32[]{:S(2)}) collective-permute-start(bf16[128,256]{1,0:T(8,128)(2,1)S(1)} %get-tuple-element.24), channel_id=1, source_target_pairs={{0,120},{8,24},{16,88},{24,56},{32,16},{40,48},{48,112},{56,80},{6... | collective-permute-start | bytes 196616 | tf_op jit(solution)/shard_map/ppermute | solution.py:336
  141.3 0.0 collective-permute-done.refs_0_
  141.3 0.0 collective-permute-done.1.refs_1_
  141.4 0.7 collective-permute-done.2.refs_2_
  142.1 4.7 %collective-permute-done.3.refs_3_ = bf16[128,256]{1,0:T(8,128)(2,1)S(1)} collective-permute-done((bf16[128,256]{1,0:T(8,128)(2,1)S(1)}, bf16[128,256]{1,0:T(8,128)(2,1)S(1)}, u32[]{:S(2)}, u32[]{:S(2)}) %collective-permute-start.3) | collective-permute-done | bytes 65568 | tf_op jit(solution)/shard_map/ppermute | solution.py:336
  146.8 0.7 shard_map.79
  (1 shorter events, 0.0 us)
Async XLA Ops:
  2.7 18.8 %copy-start = (s32[1,64,64]{2,1,0:T(8,128)S(1)}, s32[1,64,64]{2,1,0:T(8,128)}, u32[]{:S(2)}) copy-start(s32[1,64,64]{2,1,0:T(8,128)} %param.11) | copy-start | bytes 49156
  2.7 84.0 %copy-start.1 = (s32[8]{0:T(128)S(1)}, s32[8]{0:T(128)}, u32[]{:S(2)}) copy-start(s32[8]{0:T(128)} %lengths_ref.3) | copy-start | bytes 100
  2.7 84.0 %all-to-all-start = ((bf16[64,16,640]{2,1,0:T(8,128)(2,1)}), bf16[64,16,640]{2,1,0:T(8,128)(2,1)S(1)}, u32[]{:S(2)}, u32[]{:S(2)}) async-start(bf16[64,16,640]{2,1,0:T(8,128)(2,1)} %bitcast.9), calls=%async_computation | async-start | bytes 2621440 | tf_op jit(solution)/shard_map/all_to_all | solution.py:309
  86.6 27.4 %copy-start.2 = (f32[1024]{0:T(1024)S(1)}, f32[1024]{0:T(1024)}, u32[]{:S(2)}) copy-start(f32[1024]{0:T(1024)} %param.13) | copy-start | bytes 12292
  107.5 15.3 %all-to-all-start.2 = ((f32[64,1,512]{2,1,0:T(1,128)}), f32[64,1,512]{2,1,0:T(1,128)S(1)}, u32[]{:S(2)}, u32[]{:S(2)}) async-start(f32[64,1,512]{2,1,0:T(1,128)} %shard_map.76), calls=%async_computation.2 | async-start | bytes 262144 | tf_op jit(solution)/shard_map/all_to_all | solution.py:330
  123.5 17.8 %collective-permute-start = (bf16[128,256]{1,0:T(8,128)(2,1)S(1)}, bf16[128,256]{1,0:T(8,128)(2,1)S(1)}, u32[]{:S(2)}, u32[]{:S(2)}) collective-permute-start(bf16[128,256]{1,0:T(8,128)(2,1)S(1)} %get-tuple-element.21), channel_id=1, source_target_pairs={{0,96},{8,0},{16,64},{24,32},{32,8},{40,40},{48,104},{56,72},{64,4... | collective-permute-start | bytes 196616 | tf_op jit(solution)/shard_map/ppermute | solution.py:336
  127.1 14.3 %collective-permute-start.1 = (bf16[128,256]{1,0:T(8,128)(2,1)S(1)}, bf16[128,256]{1,0:T(8,128)(2,1)S(1)}, u32[]{:S(2)}, u32[]{:S(2)}) collective-permute-start(bf16[128,256]{1,0:T(8,128)(2,1)S(1)} %get-tuple-element.22), channel_id=1, source_target_pairs={{0,104},{8,8},{16,72},{24,40},{32,0},{40,32},{48,96},{56,64},{64,5... | collective-permute-start | bytes 196616 | tf_op jit(solution)/shard_map/ppermute | solution.py:336
  129.0 13.1 %collective-permute-start.2 = (bf16[128,256]{1,0:T(8,128)(2,1)S(1)}, bf16[128,256]{1,0:T(8,128)(2,1)S(1)}, u32[]{:S(2)}, u32[]{:S(2)}) collective-permute-start(bf16[128,256]{1,0:T(8,128)(2,1)S(1)} %get-tuple-element.23), channel_id=1, source_target_pairs={{0,112},{8,16},{16,80},{24,48},{32,24},{40,56},{48,120},{56,88},{6... | collective-permute-start | bytes 196616 | tf_op jit(solution)/shard_map/ppermute | solution.py:336
  139.4 7.4 %collective-permute-start.3 = (bf16[128,256]{1,0:T(8,128)(2,1)S(1)}, bf16[128,256]{1,0:T(8,128)(2,1)S(1)}, u32[]{:S(2)}, u32[]{:S(2)}) collective-permute-start(bf16[128,256]{1,0:T(8,128)(2,1)S(1)} %get-tuple-element.24), channel_id=1, source_target_pairs={{0,120},{8,24},{16,88},{24,56},{32,16},{40,48},{48,112},{56,80},{6... | collective-permute-start | bytes 196616 | tf_op jit(solution)/shard_map/ppermute | solution.py:336
